TPU v7x, 32 devices: a whole 2x2x4 slice. The times are simulated.
32 devices in a mesh: wide: 32 (over z, y, x, core).
Axes of the slice: x: 2, y: 2, z: 4, core: 2. Of those that a mesh axis runs over, the one named last changes fastest.
Arguments:
- features: bfloat16 [49152, 2048], P('wide'), may hold values from -6 to 6
- group_ids: int32 [32], P('wide'), may hold values from 0 to 3, as said below
- reducer: bfloat16 [2048, 512], replicated, may hold values from -0.125 to 0.125
- spatial: bfloat16 [4608, 512], replicated, may hold values from -0.09375 to 0.09375
- expander: bfloat16 [512, 2048], replicated, may hold values from -0.25 to 0.25
- gain_first: float32 [512], replicated, may hold values from 0.5 to 1.5
- bias_first: float32 [512], replicated, may hold values from -3 to 3
- gain_middle: float32 [512], replicated, may hold values from 0.5 to 1.5
- bias_middle: float32 [512], replicated, may hold values from -3 to 3
- gain_last: float32 [2048], replicated, may hold values from 0.5 to 1.5
- bias_last: float32 [2048], replicated, may hold values from -3 to 3
- upstream: bfloat16 [49152, 2048], P('wide'), may hold values from -6 to 6
Outputs:
- block_out: bfloat16 [49152, 2048], P('wide')
- features_grad: bfloat16 [49152, 2048], P('wide')
- reducer_grad: float32 [2048, 512], replicated
- spatial_grad: float32 [4608, 512], replicated
- expander_grad: float32 [512, 2048], replicated
- gain_first_gradient: float32 [512], replicated
- bias_first_gradient: float32 [512], replicated
- gain_middle_gradient: float32 [512], replicated
- bias_middle_gradient: float32 [512], replicated
- gain_last_gradient: float32 [2048], replicated
- bias_last_gradient: float32 [2048], replicated
Inputs may be any that keep to these rules, and one draw needn't show every extreme that they name: `group_ids`: each of the four ids is held by exactly 8 devices.
All inputs are finite; a program needn't handle non-finite values.
Results may differ from a plain program's by a relative error of at most 0.0085.
Values sent between devices are 32-bit elements; how exact they have to be, the bound alone decides.
No kernel may reach another device: no remote copies, remote signals or barrier semaphores. Data moves between devices by JAX's collectives and lax.ppermute only.
A program may use at most 192 MiB of HBM per device.

v0:
```python
import jax
import jax.numpy as jnp
from jax import lax
from jax.sharding import PartitionSpec as P

epsilon = 1e-05


def silu_slope(values):
    sigma = jax.nn.sigmoid(values)
    return sigma * (1.0 + values * (1.0 - sigma))


def contract_rows(left, right):
    return lax.dot_general(
        left, right, (((0,), (0,)), ((), ())), preferred_element_type=jnp.float32
    )


def contract_cols(left, right):
    return lax.dot_general(
        left, right, (((1,), (1,)), ((), ())), preferred_element_type=jnp.float32
    )


def layout(group_value, rows):
    side = jnp.where(group_value == 3, 2, 5 + group_value)
    area = side * side
    positions = jnp.arange(rows, dtype=jnp.int32)
    images = positions // area
    within = positions % area
    row_pos = within // side
    col_pos = within % side
    valid = (images < rows // area).astype(jnp.float32)
    shifts = []
    windows = []
    for delta_row in (-1, 0, 1):
        for delta_col in (-1, 0, 1):
            shifts.append(delta_row * side + delta_col)
            inside = (
                (row_pos + delta_row >= 0)
                & (row_pos + delta_row < side)
                & (col_pos + delta_col >= 0)
                & (col_pos + delta_col < side)
            )
            windows.append(inside.astype(jnp.float32))
    return (valid, shifts, windows)


def own_row(picker, table):
    return jnp.sum(picker[:, None] * table, axis=0)


def stream_stats(values, valid, picker):
    weighted = valid[:, None] * values
    first = jnp.sum(weighted, axis=0)
    count = jnp.sum(valid)
    totals, counts = lax.psum((picker[:, None] * first[None, :], picker * count), "wide")
    number = jnp.sum(picker * counts)
    mean = own_row(picker, totals) / number
    centered = values - mean
    spread = jnp.sum(valid[:, None] * centered * centered, axis=0)
    squares = lax.psum(picker[:, None] * spread[None, :], "wide")
    variance = own_row(picker, squares) / number
    return (mean, lax.rsqrt(variance + epsilon), number)


def norm_back(grad_norm, normed, gain, inverse, number, valid, picker):
    first = jnp.sum(grad_norm, axis=0)
    second = jnp.sum(grad_norm * normed, axis=0)
    totals, products = lax.psum(
        (picker[:, None] * first[None, :], picker[:, None] * second[None, :]), "wide"
    )
    own_total = own_row(picker, totals)
    own_product = own_row(picker, products)
    grad_in = (
        valid[:, None]
        * (gain * inverse)
        * (grad_norm - (own_total + normed * own_product) / number)
    )
    return (grad_in, jnp.sum(products, axis=0), jnp.sum(totals, axis=0))


def on_device(
    features,
    group_ids,
    reducer,
    spatial,
    expander,
    gain_first,
    bias_first,
    gain_middle,
    bias_middle,
    gain_last,
    bias_last,
    upstream,
):
    rows = features.shape[0]
    width = spatial.shape[1]
    group_value = group_ids[0]
    picker = jnp.stack([group_value != 3, group_value == 3]).astype(jnp.float32)
    valid, shifts, windows = layout(group_value, rows)
    valid_col = valid[:, None]
    pre_first = jnp.dot(features, reducer, preferred_element_type=jnp.float32)
    mean_first, inverse_first, number_first = stream_stats(pre_first, valid, picker)
    normed_first = (pre_first - mean_first) * inverse_first
    act_first = normed_first * gain_first + bias_first
    low_first = (jax.nn.silu(act_first) * valid_col).astype(jnp.bfloat16)
    columns = jnp.concatenate(
        [
            jnp.roll(low_first, -shifts[tap_index], axis=0)
            * windows[tap_index][:, None].astype(jnp.bfloat16)
            for tap_index in range(9)
        ],
        axis=1,
    )
    pre_middle = jnp.dot(columns, spatial, preferred_element_type=jnp.float32)
    mean_middle, inverse_middle, number_middle = stream_stats(pre_middle, valid, picker)
    normed_middle = (pre_middle - mean_middle) * inverse_middle
    act_middle = normed_middle * gain_middle + bias_middle
    low_middle = (jax.nn.silu(act_middle) * valid_col).astype(jnp.bfloat16)
    pre_last = jnp.dot(low_middle, expander, preferred_element_type=jnp.float32)
    mean_last, inverse_last, number_last = stream_stats(pre_last, valid, picker)
    normed_last = (pre_last - mean_last) * inverse_last
    act_last = normed_last * gain_last + bias_last
    summed = act_last + features.astype(jnp.float32)
    block_out = (jax.nn.silu(summed) * valid_col).astype(jnp.bfloat16)
    grad_summed = upstream.astype(jnp.float32) * valid_col * silu_slope(summed)
    grad_pre_last, gain_last_gradient, bias_last_gradient = norm_back(
        grad_summed, normed_last, gain_last, inverse_last, number_last, valid, picker
    )
    low_grad_last = grad_pre_last.astype(jnp.bfloat16)
    expander_grad = contract_rows(low_middle, low_grad_last)
    grad_low_middle = contract_cols(low_grad_last, expander)
    grad_act_middle = grad_low_middle * valid_col * silu_slope(act_middle)
    grad_pre_middle, gain_middle_gradient, bias_middle_gradient = norm_back(
        grad_act_middle, normed_middle, gain_middle, inverse_middle, number_middle, valid, picker
    )
    low_grad_middle = grad_pre_middle.astype(jnp.bfloat16)
    spatial_grad = contract_rows(columns, low_grad_middle)
    grad_columns = contract_cols(low_grad_middle, spatial)
    grad_low_first = jnp.zeros((rows, width), jnp.float32)
    for tap_index in range(9):
        block = (
            grad_columns[:, tap_index * width : (tap_index + 1) * width]
            * windows[tap_index][:, None]
        )
        grad_low_first = grad_low_first + jnp.roll(block, shifts[tap_index], axis=0)
    grad_act_first = grad_low_first * valid_col * silu_slope(act_first)
    grad_pre_first, gain_first_gradient, bias_first_gradient = norm_back(
        grad_act_first, normed_first, gain_first, inverse_first, number_first, valid, picker
    )
    low_grad_first = grad_pre_first.astype(jnp.bfloat16)
    reducer_grad = contract_rows(features, low_grad_first)
    features_grad = (contract_cols(low_grad_first, reducer) + grad_summed).astype(jnp.bfloat16)
    reducer_grad, spatial_grad, expander_grad = lax.psum(
        (reducer_grad, spatial_grad, expander_grad), "wide"
    )
    return (
        block_out,
        features_grad,
        reducer_grad,
        spatial_grad,
        expander_grad,
        gain_first_gradient,
        bias_first_gradient,
        gain_middle_gradient,
        bias_middle_gradient,
        gain_last_gradient,
        bias_last_gradient,
    )


def solution(mesh):
    in_specs = (
        P("wide", None),
        P("wide"),
        P(),
        P(),
        P(),
        P(),
        P(),
        P(),
        P(),
        P(),
        P(),
        P("wide", None),
    )
    out_specs = (P("wide", None), P("wide", None), P(), P(), P(), P(), P(), P(), P(), P(), P())
    return jax.shard_map(
        on_device, mesh=mesh, in_specs=in_specs, out_specs=out_specs, check_vma=False
    )
```

profile of v0, /device:TPU:0, one launch (start us, length us, event | category | flops | bytes accessed | tf_op | source)
XLA Modules:
  0.0 874.0 jit_solution(11407308439564908342)
XLA Ops:
  8.3 0.7 fusion.57
  9.5 0.9 and_convert_fusion.8
  11.7 0.9 and_convert_fusion
  12.7 0.9 and_convert_fusion.2
  13.6 0.9 and_convert_fusion.6
  14.5 0.9 and_convert_fusion.4
  15.5 0.7 broadcast_select_fusion
  16.3 8.5 multiply_reduce_fusion.5
  24.9 42.0 %all-reduce.3 = (f32[2,512]{1,0:T(2,128)S(1)}, f32[2]{0:T(128)S(1)}) all-reduce(f32[2,512]{1,0:T(2,128)S(1)} %broadcast_multiply_fusion.11, f32[2]{0:T(128)S(1)} %broadcast_select_fusion), channel_id=1, replica_groups=mesh['wide'=32] {'wide'}, use_global_device_ids=true, to_apply=%region_1.2 | all-reduce | flops 1026 | bytes 8208 | tf_op jit(solution)/shard_map/psum | solution.py:58
  66.9 0.7 select_reduce_fusion
  68.3 2.4 fusion.2
  70.8 40.6 %psum.120 = f32[2,512]{1,0:T(2,128)S(1)} all-reduce(f32[2,512]{1,0:T(2,128)S(1)} %broadcast_multiply_fusion.10), channel_id=1, replica_groups=mesh['wide'=32] {'wide'}, use_global_device_ids=true, to_apply=%region_7.8 | all-reduce | flops 1024 | bytes 8192 | tf_op jit(solution)/shard_map/psum | solution.py:63
  111.5 1.2 fusion.79
  112.7 3.0 multiply_convert_fusion.5
  115.6 1.5 fusion.25
  117.1 1.5 fusion.28
  118.7 1.5 fusion.31
  120.7 1.8 multiply_dynamic-update-slice_fusion
  123.0 1.5 fusion.40
  124.5 1.5 fusion.43
  126.0 1.5 fusion.22
  127.5 9.4 %multiply_reduce_fusion.4 = (f32[512]{0:T(512)S(1)}, f32[1536,512]{1,0:T(8,128)}) fusion(f32[1536]{0:T(1024)S(1)} %fusion.50, bf16[1536,4608]{1,0:T(8,128)(2,1)S(1)} %fusion.22, bf16[4608,512]{1,0:T(8,128)(2,1)S(1)} %bitcast.20), kind=kOutput, calls=%fused_computation.80 | convolution fusion | flops 7249329664 | bytes 22028288 | tf_op jit(solution)/shard_map/dot_general | solution.py:117
  137.0 40.0 %psum.121 = f32[2,512]{1,0:T(2,128)S(1)} all-reduce(f32[2,512]{1,0:T(2,128)S(1)} %broadcast_multiply_fusion.9), channel_id=1, replica_groups=mesh['wide'=32] {'wide'}, use_global_device_ids=true, to_apply=%region_10.15 | all-reduce | flops 1024 | bytes 8192 | tf_op jit(solution)/shard_map/psum | solution.py:58
  177.7 2.4 fusion.3
  180.2 40.3 %psum.122 = f32[2,512]{1,0:T(2,128)S(1)} all-reduce(f32[2,512]{1,0:T(2,128)S(1)} %broadcast_multiply_fusion.8), channel_id=1, replica_groups=mesh['wide'=32] {'wide'}, use_global_device_ids=true, to_apply=%region_13.18 | all-reduce | flops 1024 | bytes 8192 | tf_op jit(solution)/shard_map/psum | solution.py:63
  221.2 8.5 multiply_reduce_fusion.1
  229.8 40.0 %psum.123 = f32[2,2048]{1,0:T(2,128)S(1)} all-reduce(f32[2,2048]{1,0:T(2,128)S(1)} %broadcast_multiply_fusion.3), channel_id=1, replica_groups=mesh['wide'=32] {'wide'}, use_global_device_ids=true, to_apply=%region_16.21 | all-reduce | flops 4096 | bytes 32768 | tf_op jit(solution)/shard_map/psum | solution.py:58
  270.6 6.3 fusion
  277.0 40.1 %psum.124 = f32[2,2048]{1,0:T(2,128)S(1)} all-reduce(f32[2,2048]{1,0:T(2,128)S(1)} %broadcast_multiply_fusion.2), channel_id=1, replica_groups=mesh['wide'=32] {'wide'}, use_global_device_ids=true, to_apply=%region_19.24 | all-reduce | flops 4096 | bytes 32768 | tf_op jit(solution)/shard_map/psum | solution.py:63
  317.9 20.7 %fusion.70 = (f32[2048]{0:T(1024)S(1)}, f32[2048]{0:T(1024)S(1)}, f32[1536,2048]{1,0:T(8,128)}, bf16[1536,2048]{1,0:T(8,128)(2,1)}) fusion(f32[2048]{0:T(1024)S(1)} %get-tuple-element.76, f32[1536,2048]{1,0:T(8,128)} %get-tuple-element.104, f32[2048]{0:T(1024)S(1)} %broadcast_divide_fusion, bf16[1536,2048]{1,0:T(8,128)(2,1)} %param.28, ...), kind=kLoop, calls=%fused_computation.198 | loop fusion | flops 69201920 | bytes 44095488 | tf_op jit(solution)/shard_map/reduce_sum | solution.py:69
  338.6 40.6 %all-reduce.2 = (f32[2,2048]{1,0:T(2,128)S(1)}, f32[2,2048]{1,0:T(2,128)S(1)}) all-reduce(f32[2,2048]{1,0:T(2,128)S(1)} %get-tuple-element.98, f32[2,2048]{1,0:T(2,128)S(1)} %get-tuple-element.97), channel_id=1, replica_groups=mesh['wide'=32] {'wide'}, use_global_device_ids=true, to_apply=%region_25.30 | all-reduce | flops 8192 | bytes 65536 | tf_op jit(solution)/shard_map/psum | solution.py:71
  379.9 10.8 %multiply_convert_fusion = bf16[1536,2048]{1,0:T(8,128)(2,1)S(1)} fusion(f32[1536,2048]{1,0:T(8,128)} %get-tuple-element.77, f32[1536,2048]{1,0:T(8,128)} %get-tuple-element.104, f32[]{:T(128)} %select_reduce_fusion, f32[2048]{0:T(1024)S(1)} %get-tuple-element.95, f32[2048]{0:T(1024)S(1)} %get-tuple-element.48, f32[2048]{0:T(1024)S(1)} %get-tuple-element.75, ...), kind=kLoop, calls=%fused_computation.3 | loop fusion | flops 28311552 | bytes 31504388 | tf_op jit(solution)/shard_map/convert_element_type | solution.py:132
  390.7 6.9 fusion.72
  397.6 5.3 fusion.68
  402.9 40.3 %all-reduce.1 = (f32[2,512]{1,0:T(2,128)S(1)}, f32[2,512]{1,0:T(2,128)S(1)}) all-reduce(f32[2,512]{1,0:T(2,128)S(1)} %get-tuple-element.94, f32[2,512]{1,0:T(2,128)S(1)} %get-tuple-element.93), channel_id=1, replica_groups=mesh['wide'=32] {'wide'}, use_global_device_ids=true, to_apply=%region_31.36 | all-reduce | flops 2048 | bytes 16384 | tf_op jit(solution)/shard_map/psum | solution.py:71
  443.8 4.7 multiply_convert_fusion.3
  448.5 13.0 %fusion.84 = f32[4608,512]{1,0:T(8,128)} fusion(bf16[1536,4608]{1,0:T(8,128)(2,1)} %copy-done.6, bf16[1536,512]{1,0:T(8,128)(2,1)S(1)} %multiply_convert_fusion.3), kind=kOutput, calls=%fused_computation.211 | convolution fusion | flops 7247757312 | bytes 25165824 | tf_op jit(solution)/shard_map/dot_general | solution.py:15
  461.6 12.7 %fusion.83 = f32[1536,4608]{1,0:T(8,128)} fusion(bf16[1536,512]{1,0:T(8,128)(2,1)S(1)} %multiply_convert_fusion.3, bf16[4608,512]{1,0:T(8,128)(2,1)S(1)} %bitcast.22), kind=kOutput, calls=%fused_computation.210 | convolution fusion | flops 7247757312 | bytes 34603008 | tf_op jit(solution)/shard_map/dot_general | solution.py:21
  474.4 14.5 %slice_multiply_fusion.8 = (f32[1536,512]{1,0:T(8,128)S(1)}, f32[1536,512]{1,0:T(8,128)S(1)}, f32[1536,512]{1,0:T(8,128)S(1)}, f32[1536,512]{1,0:T(8,128)S(1)}, ...) fusion(f32[1536,4608]{1,0:T(8,128)} %fusion.83, ...), kind=kLoop, calls=%fused_computation.72 | loop fusion | flops 6291456 | bytes 50380800 | tf_op jit(solution)/shard_map/mul | solution.py:145
  489.0 16.7 %fusion.71 = (f32[512]{0:T(512)S(1)}, f32[512]{0:T(512)S(1)}, f32[1536,512]{1,0:T(8,128)}) fusion(f32[512]{0:T(512)S(1)} %copy-done.10, f32[1536,512]{1,0:T(8,128)S(1)} %copy-done.3, f32[512]{0:T(512)S(1)} %copy-done.8, f32[512]{0:T(512)S(1)} %copy-done.24, f32[512]{0:T(512)S(1)} %copy-done.12, f32[1536]{0:T(1024)S(1)} %fusion.50, s32[]{:T(128)S(6)} %select_n.289, ...), kind=kLoop, calls=%fused_computation.199 | loop fusion | flops 25951232 | bytes 34627608 | tf_op jit(solution)/shard_map/reduce_sum | solution.py:69
  505.7 40.1 %all-reduce = (f32[2,512]{1,0:T(2,128)S(1)}, f32[2,512]{1,0:T(2,128)S(1)}) all-reduce(f32[2,512]{1,0:T(2,128)S(1)} %get-tuple-element.90, f32[2,512]{1,0:T(2,128)S(1)} %get-tuple-element.89), channel_id=1, replica_groups=mesh['wide'=32] {'wide'}, use_global_device_ids=true, to_apply=%region_37.46 | all-reduce | flops 2048 | bytes 16384 | tf_op jit(solution)/shard_map/psum | solution.py:71
  546.4 4.4 multiply_convert_fusion.2
  550.7 7.8 convolution_bitcast_fusion
  558.5 8.8 %add_convert_fusion = bf16[1536,2048]{1,0:T(8,128)(2,1)} fusion(f32[1536,2048]{1,0:T(8,128)} %get-tuple-element.77, bf16[1536,512]{1,0:T(8,128)(2,1)S(1)} %multiply_convert_fusion.2, bf16[2048,512]{1,0:T(8,128)(2,1)} %param.30), kind=kOutput, calls=%fused_computation.2 | convolution fusion | flops 3227516928 | bytes 22544384 | tf_op jit(solution)/shard_map/dot_general | solution.py:21
  567.3 283.5 %all-reduce.7.cloned.1.call-done = (f32[2048,512]{0,1:T(8,128)}, f32[4608,512]{1,0:T(8,128)}, f32[512,2048]{1,0:T(8,128)}) async-done(((f32[2048,512]{0,1:T(8,128)}, f32[4608,512]{1,0:T(8,128)}, f32[512,2048]{1,0:T(8,128)}), (f32[2048,512]{0,1:T(8,128)}, f32[4608,512]{1,0:T(8,128)}, f32[512,2048]{1,0:T(8,128)})) %all-reduce.7.cloned.1.call-update) | async-done | bytes 17825808 | tf_op jit(solution)/shard_map/psum | solution.py:156
  850.8 5.3 copy.24
  856.1 8.8 %copy.37 = f32[4608,512]{1,0:T(8,128)} copy(f32[4608,512]{1,0:T(8,128)} %get-tuple-element.125) | data formatting | bytes 18874368
  864.9 2.0 copy.38
  (102 shorter events, 9.3 us)
Async XLA Ops:
  7.2 214.0 %copy-start = (bf16[512,2048]{1,0:T(8,128)(2,1)S(1)}, bf16[512,2048]{1,0:T(8,128)(2,1)}, u32[]{:S(2)}) copy-start(bf16[512,2048]{1,0:T(8,128)(2,1)} %param.32) | copy-start | bytes 6291460
  7.2 843.6 %all-reduce.7.cloned.1.call-start = ((), (), s32[]{:S(2)}) async-start(), calls=%async_computation | async-start | bytes 35651584 | tf_op jit(solution)/shard_map/psum | solution.py:156
  24.8 86.7 %copy-start.11 = (f32[512]{0:T(512)S(1)}, f32[512]{0:T(512)}, u32[]{:S(2)}) copy-start(f32[512]{0:T(512)} %param.33) | copy-start | bytes 6148
  24.8 87.9 %copy-start.23 = (f32[512]{0:T(512)S(1)}, f32[512]{0:T(512)}, u32[]{:S(2)}) copy-start(f32[512]{0:T(512)} %param.34) | copy-start | bytes 6148
  68.3 52.3 %copy-start.7 = (f32[512]{0:T(512)}, f32[512]{0:T(512)S(1)}, u32[]{:S(2)}) copy-start(f32[512]{0:T(512)S(1)} %broadcast_divide_fusion.2) | copy-start | bytes 6148
  112.7 8.0 copy-start.9
  118.6 2.0 copy-start.2
  120.7 6.8 slice-start
  123.0 4.5 slice-start.1
  127.5 9.4 %copy-start.6 = (bf16[1536,4608]{1,0:T(8,128)(2,1)}, bf16[1536,4608]{1,0:T(8,128)(2,1)S(1)}, u32[]{:S(2)}) copy-start(bf16[1536,4608]{1,0:T(8,128)(2,1)S(1)} %fusion.22) | copy-start | bytes 42467332
  137.0 83.6 %copy-start.27 = (f32[512]{0:T(512)S(1)}, f32[512]{0:T(512)}, u32[]{:S(2)}) copy-start(f32[512]{0:T(512)} %param.35) | copy-start | bytes 6148
  137.0 84.3 %copy-start.28 = (f32[512]{0:T(512)S(1)}, f32[512]{0:T(512)}, u32[]{:S(2)}) copy-start(f32[512]{0:T(512)} %param.36) | copy-start | bytes 6148
  270.6 46.6 %copy-start.21 = (f32[2048]{0:T(1024)S(1)}, f32[2048]{0:T(1024)}, u32[]{:S(2)}) copy-start(f32[2048]{0:T(1024)} %param.37) | copy-start | bytes 24580
  270.6 47.3 %copy-start.25 = (f32[2048]{0:T(1024)S(1)}, f32[2048]{0:T(1024)}, u32[]{:S(2)}) copy-start(f32[2048]{0:T(1024)} %param.38) | copy-start | bytes 24580
  379.9 10.8 %copy-start.4 = (f32[1536,512]{1,0:T(8,128)S(1)}, f32[1536,512]{1,0:T(8,128)}, u32[]{:S(2)}) copy-start(f32[1536,512]{1,0:T(8,128)} %get-tuple-element.102) | copy-start | bytes 9437188
  443.8 17.7 %slice-start.2 = ((s8[4718592]{0:T(1024)(128)(4,1)}), s8[4194304]{0:T(1024)(128)(4,1)S(1)}, s32[]{:S(2)}) async-start(s8[4718592]{0:T(1024)(128)(4,1)} %bitcast.21), calls=%async_computation.3 | async-start | bytes 8388608
  448.5 13.0 %slice-start.3 = ((s8[4718592]{0:T(1024)(128)(4,1)}), s8[524288]{0:T(1024)(128)(4,1)S(1)}, s32[]{:S(2)}) async-start(s8[4718592]{0:T(1024)(128)(4,1)} %bitcast.21), calls=%async_computation.4 | async-start | bytes 1048576
  461.5 12.7 %copy-start.13 = (f32[1536]{0:T(1024)S(1)}, f32[1536]{0:T(1024)}, u32[]{:S(2)}) copy-start(f32[1536]{0:T(1024)} %and_convert_fusion.8) | copy-start | bytes 18436
  461.5 12.7 %copy-start.14 = (f32[1536]{0:T(1024)S(1)}, f32[1536]{0:T(1024)}, u32[]{:S(2)}) copy-start(f32[1536]{0:T(1024)} %get-tuple-element.106) | copy-start | bytes 18436
  461.5 12.7 %copy-start.15 = (f32[1536]{0:T(1024)S(1)}, f32[1536]{0:T(1024)}, u32[]{:S(2)}) copy-start(f32[1536]{0:T(1024)} %get-tuple-element.107) | copy-start | bytes 18436
  461.5 12.7 %copy-start.16 = (f32[1536]{0:T(1024)S(1)}, f32[1536]{0:T(1024)}, u32[]{:S(2)}) copy-start(f32[1536]{0:T(1024)} %get-tuple-element.108) | copy-start | bytes 18436
  461.5 12.7 %copy-start.17 = (f32[1536]{0:T(1024)S(1)}, f32[1536]{0:T(1024)}, u32[]{:S(2)}) copy-start(f32[1536]{0:T(1024)} %get-tuple-element.109) | copy-start | bytes 18436
  461.6 12.7 %copy-start.18 = (f32[1536]{0:T(1024)S(1)}, f32[1536]{0:T(1024)}, u32[]{:S(2)}) copy-start(f32[1536]{0:T(1024)} %get-tuple-element.112) | copy-start | bytes 18436
  461.6 12.7 %copy-start.19 = (f32[1536]{0:T(1024)S(1)}, f32[1536]{0:T(1024)}, u32[]{:S(2)}) copy-start(f32[1536]{0:T(1024)} %get-tuple-element.113) | copy-start | bytes 18436
  461.6 12.7 %copy-start.20 = (f32[1536]{0:T(1024)S(1)}, f32[1536]{0:T(1024)}, u32[]{:S(2)}) copy-start(f32[1536]{0:T(1024)} %get-tuple-element.111) | copy-start | bytes 18436
  474.3 14.6 %copy-start.3 = (f32[1536,512]{1,0:T(8,128)S(1)}, f32[1536,512]{1,0:T(8,128)}, u32[]{:S(2)}) copy-start(f32[1536,512]{1,0:T(8,128)} %get-tuple-element.100) | copy-start | bytes 9437188
  474.3 14.6 %copy-start.8 = (f32[512]{0:T(512)S(1)}, f32[512]{0:T(512)}, u32[]{:S(2)}) copy-start(f32[512]{0:T(512)} %copy-done.7) | copy-start | bytes 6148
  474.3 14.6 %copy-start.10 = (f32[512]{0:T(512)S(1)}, f32[512]{0:T(512)}, u32[]{:S(2)}) copy-start(f32[512]{0:T(512)} %copy-done.9) | copy-start | bytes 6148
  474.3 14.6 %copy-start.12 = (f32[512]{0:T(512)S(1)}, f32[512]{0:T(512)}, u32[]{:S(2)}) copy-start(f32[512]{0:T(512)} %param.33) | copy-start | bytes 6148
  474.4 14.6 %copy-start.22 = (f32[1536]{0:T(1024)S(1)}, f32[1536]{0:T(1024)}, u32[]{:S(2)}) copy-start(f32[1536]{0:T(1024)} %get-tuple-element.110) | copy-start | bytes 18436
  474.4 14.6 %copy-start.24 = (f32[512]{0:T(512)S(1)}, f32[512]{0:T(512)}, u32[]{:S(2)}) copy-start(f32[512]{0:T(512)} %param.34) | copy-start | bytes 6148
  488.9 57.4 %copy-start.26 = (f32[512]{0:T(512)S(1)}, f32[512]{0:T(512)}, u32[]{:S(2)}) copy-start(f32[512]{0:T(512)} %get-tuple-element.70) | copy-start | bytes 6148
  856.1 8.8 %copy-start.5 = (f32[512,2048]{1,0:T(8,128)S(1)}, f32[512,2048]{1,0:T(8,128)}, u32[]{:S(2)}) copy-start(f32[512,2048]{1,0:T(8,128)} %get-tuple-element.126) | copy-start | bytes 12582916
  856.1 10.8 %copy-start.1 = (bf16[512,2048]{1,0:T(8,128)(2,1)S(1)}, bf16[512,2048]{1,0:T(8,128)(2,1)}, u32[]{:S(2)}) copy-start(bf16[512,2048]{1,0:T(8,128)(2,1)} %param.32) | copy-start | bytes 6291460
Sparse Core Ops, SparseCore 0:
  558.7 292.0 all-reduce.6
where the time goes:
time: 882 us; the launch traced here: 874 us
  blocking collectives  364 us (41%)
  waiting for transfers between devices  283 us (32%)
  other arithmetic  113 us (13%)
  matrix products  80.8 us (9%)
  local copies, waits for them, and re-layouts  16.3 us (2%)
  between operations  15.9 us (2%)
    psum x1, waiting for transfers between devices, on_device(): lax.psum((reducer_grad, spatial_grad, expander_grad), 'wide')  283 us
    psum x3, blocking collectives, stream_stats(): lax.psum((picker[:, None] * first[None, :], picker * count), 'wide')  122 us
    psum x3, blocking collectives, stream_stats(): squares = lax.psum(picker[:, None] * spread[None, :], 'wide')  121 us
    psum x3, blocking collectives, norm_back(): lax.psum((picker[:, None] * first[None, :], picker[:, None] * second[None...  121 us
    reduce_sum x2, other arithmetic, norm_back(): first = jnp.sum(grad_norm, axis=0)  37.3 us
    dot_general x3, matrix products, contract_cols(): lax.dot_general(left, right, (((1,), (1,)), ((), ())), preferred_element_...  28.3 us
    dot_general x3, matrix products, contract_rows(): lax.dot_general(left, right, (((0,), (0,)), ((), ())), preferred_element_...  26.1 us
  transfers between devices with their start and end apart: 1, of which 1 were waited for; matrix products, arithmetic and copies ran while one was open for 1% of the time, Pallas kernels for 0%

commit v1 on v0

--- a/solution.py
+++ b/solution.py
@@ -51,26 +51,76 @@
     return jnp.sum(picker[:, None] * table, axis=0)
 
 
-def stream_stats(values, valid, picker):
-    weighted = valid[:, None] * values
-    first = jnp.sum(weighted, axis=0)
-    count = jnp.sum(valid)
-    totals, counts = lax.psum((picker[:, None] * first[None, :], picker * count), "wide")
-    number = jnp.sum(picker * counts)
-    mean = own_row(picker, totals) / number
+class Wide:
+    def __init__(self, devices):
+        self.devices = devices
+        self.bits = [1 << k for k in range(devices.bit_length() - 1)]
+
+    def swap(self, value, bit):
+        pairs = [(i, i ^ bit) for i in range(self.devices)]
+        return lax.ppermute(value, "wide", pairs)
+
+    def high(self, bit):
+        return (lax.axis_index("wide") & bit) != 0
+
+    def total(self, value):
+        for bit in self.bits:
+            value = value + self.swap(value, bit)
+        return value
+
+    def merge_counts(self, counts):
+        stages = []
+        for bit in self.bits:
+            other = self.swap(counts, bit)
+            stages.append((counts, other))
+            counts = counts + other
+        return stages, counts
+
+    def merge_moments(self, mean, square, stages):
+        for bit, (own, other) in zip(self.bits, stages):
+            packed = self.swap(jnp.concatenate([mean, square], axis=0), bit)
+            gap = packed[:2] - mean
+            share = other / jnp.maximum(own + other, 1.0)
+            mean = mean + gap * share[:, None]
+            square = square + packed[2:] + gap * gap * (own * share)[:, None]
+        return mean, square
+
+    def sum_replicated(self, value):
+        for bit in self.bits:
+            half = value.shape[0] // 2
+            place = self.high(bit).astype(jnp.int32)
+            sent = lax.dynamic_slice_in_dim(value, (1 - place) * half, half)
+            kept = lax.dynamic_slice_in_dim(value, place * half, half)
+            value = kept + self.swap(sent, bit)
+        for bit in self.bits[::-1]:
+            other = self.swap(value, bit)
+            up = self.high(bit)
+            value = jnp.concatenate(
+                [jnp.where(up, other, value), jnp.where(up, value, other)], axis=0
+            )
+        return value
+
+
+def stream_stats(values, valid, picker, wide, stages, number):
+    own_count = jnp.sum(valid)
+    weights = valid[:, None]
+    mean = jnp.sum(weights * values, axis=0) / own_count
     centered = values - mean
-    spread = jnp.sum(valid[:, None] * centered * centered, axis=0)
-    squares = lax.psum(picker[:, None] * spread[None, :], "wide")
+    square = jnp.sum(weights * centered * centered, axis=0)
+    means, squares = wide.merge_moments(
+        picker[:, None] * mean[None, :], picker[:, None] * square[None, :], stages
+    )
     variance = own_row(picker, squares) / number
-    return (mean, lax.rsqrt(variance + epsilon), number)
-
-
-def norm_back(grad_norm, normed, gain, inverse, number, valid, picker):
+    return (own_row(picker, means), lax.rsqrt(variance + epsilon))
+
+
+def norm_back(grad_norm, normed, gain, inverse, number, valid, picker, wide):
     first = jnp.sum(grad_norm, axis=0)
     second = jnp.sum(grad_norm * normed, axis=0)
-    totals, products = lax.psum(
-        (picker[:, None] * first[None, :], picker[:, None] * second[None, :]), "wide"
-    )
+    sums = wide.total(
+        jnp.concatenate([picker[:, None] * first[None, :], picker[:, None] * second[None, :]])
+    )
+    totals, products = sums[:2], sums[2:]
     own_total = own_row(picker, totals)
     own_product = own_row(picker, products)
     grad_in = (
@@ -82,6 +132,7 @@
 
 
 def on_device(
+    wide,
     features,
     group_ids,
     reducer,
@@ -101,8 +152,10 @@
     picker = jnp.stack([group_value != 3, group_value == 3]).astype(jnp.float32)
     valid, shifts, windows = layout(group_value, rows)
     valid_col = valid[:, None]
+    stages, counts = wide.merge_counts(picker * jnp.sum(valid))
+    number = jnp.sum(picker * counts)
     pre_first = jnp.dot(features, reducer, preferred_element_type=jnp.float32)
-    mean_first, inverse_first, number_first = stream_stats(pre_first, valid, picker)
+    mean_first, inverse_first = stream_stats(pre_first, valid, picker, wide, stages, number)
     normed_first = (pre_first - mean_first) * inverse_first
     act_first = normed_first * gain_first + bias_first
     low_first = (jax.nn.silu(act_first) * valid_col).astype(jnp.bfloat16)
@@ -115,29 +168,29 @@
         axis=1,
     )
     pre_middle = jnp.dot(columns, spatial, preferred_element_type=jnp.float32)
-    mean_middle, inverse_middle, number_middle = stream_stats(pre_middle, valid, picker)
+    mean_middle, inverse_middle = stream_stats(pre_middle, valid, picker, wide, stages, number)
     normed_middle = (pre_middle - mean_middle) * inverse_middle
     act_middle = normed_middle * gain_middle + bias_middle
     low_middle = (jax.nn.silu(act_middle) * valid_col).astype(jnp.bfloat16)
     pre_last = jnp.dot(low_middle, expander, preferred_element_type=jnp.float32)
-    mean_last, inverse_last, number_last = stream_stats(pre_last, valid, picker)
+    mean_last, inverse_last = stream_stats(pre_last, valid, picker, wide, stages, number)
     normed_last = (pre_last - mean_last) * inverse_last
     act_last = normed_last * gain_last + bias_last
     summed = act_last + features.astype(jnp.float32)
     block_out = (jax.nn.silu(summed) * valid_col).astype(jnp.bfloat16)
     grad_summed = upstream.astype(jnp.float32) * valid_col * silu_slope(summed)
     grad_pre_last, gain_last_gradient, bias_last_gradient = norm_back(
-        grad_summed, normed_last, gain_last, inverse_last, number_last, valid, picker
+        grad_summed, normed_last, gain_last, inverse_last, number, valid, picker, wide
     )
     low_grad_last = grad_pre_last.astype(jnp.bfloat16)
-    expander_grad = contract_rows(low_middle, low_grad_last)
+    expander_grad = lax.psum(contract_rows(low_middle, low_grad_last), "wide")
     grad_low_middle = contract_cols(low_grad_last, expander)
     grad_act_middle = grad_low_middle * valid_col * silu_slope(act_middle)
     grad_pre_middle, gain_middle_gradient, bias_middle_gradient = norm_back(
-        grad_act_middle, normed_middle, gain_middle, inverse_middle, number_middle, valid, picker
+        grad_act_middle, normed_middle, gain_middle, inverse_middle, number, valid, picker, wide
     )
     low_grad_middle = grad_pre_middle.astype(jnp.bfloat16)
-    spatial_grad = contract_rows(columns, low_grad_middle)
+    spatial_grad = wide.sum_replicated(contract_rows(columns, low_grad_middle))
     grad_columns = contract_cols(low_grad_middle, spatial)
     grad_low_first = jnp.zeros((rows, width), jnp.float32)
     for tap_index in range(9):
@@ -148,14 +201,11 @@
         grad_low_first = grad_low_first + jnp.roll(block, shifts[tap_index], axis=0)
     grad_act_first = grad_low_first * valid_col * silu_slope(act_first)
     grad_pre_first, gain_first_gradient, bias_first_gradient = norm_back(
-        grad_act_first, normed_first, gain_first, inverse_first, number_first, valid, picker
+        grad_act_first, normed_first, gain_first, inverse_first, number, valid, picker, wide
     )
     low_grad_first = grad_pre_first.astype(jnp.bfloat16)
-    reducer_grad = contract_rows(features, low_grad_first)
+    reducer_grad = wide.sum_replicated(contract_rows(features, low_grad_first))
     features_grad = (contract_cols(low_grad_first, reducer) + grad_summed).astype(jnp.bfloat16)
-    reducer_grad, spatial_grad, expander_grad = lax.psum(
-        (reducer_grad, spatial_grad, expander_grad), "wide"
-    )
     return (
         block_out,
         features_grad,
@@ -172,6 +222,7 @@
 
 
 def solution(mesh):
+    wide = Wide(mesh.shape["wide"])
     in_specs = (
         P("wide", None),
         P("wide"),
@@ -187,6 +238,8 @@
         P("wide", None),
     )
     out_specs = (P("wide", None), P("wide", None), P(), P(), P(), P(), P(), P(), P(), P(), P())
-    return jax.shard_map(
-        on_device, mesh=mesh, in_specs=in_specs, out_specs=out_specs, check_vma=False
-    )
+
+    def body(*arrays):
+        return on_device(wide, *arrays)
+
+    return jax.shard_map(body, mesh=mesh, in_specs=in_specs, out_specs=out_specs, check_vma=False)

time: 882 us -> 676 us (0.77)
  blocking collectives: 364 us -> 0 us
  starting transfers between devices: 0.04 us -> 67.2 us
  waiting for transfers between devices: 283 us -> 331 us
  other arithmetic: 113 us -> 149 us
  local copies, waits for them, and re-layouts: 16.3 us -> 28.1 us
    psum x9 -> x0, blocking collectives: 364 us -> none  [the longest x3 122 us: stream_stats(): lax.psum((picker[:, None] * first[None, :], picker * count), 'wide')]
    ppermute x0 -> x55, waiting for transfers between devices: none -> 227 us  [swap(): return lax.ppermute(value, 'wide', pairs)]
    psum x1, waiting for transfers between devices: 283 us -> 103 us  [on_device(): expander_grad = lax.psum(contract_rows(low_middle, low_grad_last), 'wide')]
    ppermute x0 -> x55, starting transfers between devices: none -> 67.2 us  [swap(): return lax.ppermute(value, 'wide', pairs)]
    concatenate x0 -> x28, other arithmetic: none -> 17.3 us  [the longest x10 17 us: sum_replicated(): jnp.concatenate([jnp.where(up, other, value), jnp.where(up, value, other)...]
    add x0 -> x37, other arithmetic: none -> 15.8 us  [the longest x10 12 us: sum_replicated(): value = kept + self.swap(sent, bit)]
    select_n x0 -> x10, other arithmetic: none -> 13.8 us  [sum_replicated(): jnp.where(up, other, value)]
    unnamed x69 -> x112, local copies, waits for them, and re-layouts: 16.3 us -> 20.6 us
  transfers between devices with their start and end apart: 1 -> 56, of which waited for: 1 -> 44; matrix products, arithmetic and copies ran while one was open for 1% -> 19% of each run, Pallas kernels for 0% -> 0%
where the time goes in v1:
time: 676 us; the launch traced here: 666 us
  waiting for transfers between devices  331 us (49%)
  other arithmetic  149 us (22%)
  matrix products  74.6 us (11%)
  starting transfers between devices  67.2 us (10%)
  local copies, waits for them, and re-layouts  28.1 us (4%)
  between operations  16.5 us (2%)
    ppermute x55, waiting for transfers between devices, swap(): return lax.ppermute(value, 'wide', pairs)  227 us
    psum x1, waiting for transfers between devices, on_device(): expander_grad = lax.psum(contract_rows(low_middle, low_grad_last), 'wide')  103 us
    ppermute x55, starting transfers between devices, swap(): return lax.ppermute(value, 'wide', pairs)  67.2 us
    dot_general x3, matrix products, contract_cols(): lax.dot_general(left, right, (((1,), (1,)), ((), ())), preferred_element_...  34.4 us
    reduce_sum x2, other arithmetic, norm_back(): first = jnp.sum(grad_norm, axis=0)  33.2 us
    dot_general x3, matrix products, contract_rows(): lax.dot_general(left, right, (((0,), (0,)), ((), ())), preferred_element_...  21.9 us
    unnamed x112, local copies, waits for them, and re-layouts  20.6 us
    concatenate x10, other arithmetic, sum_replicated(): jnp.concatenate([jnp.where(up, other, value), jnp.where(up, value, other)...  17 us
  transfers between devices with their start and end apart: 56, of which 44 were waited for; matrix products, arithmetic and copies ran while one was open for 19% of the time, Pallas kernels for 0%

profile of v1, /device:TPU:0, one launch (start us, length us, event | category | flops | bytes accessed | tf_op | source)
XLA Modules:
  0.0 666.4 jit_solution(16689227098933897593)
XLA Ops:
  9.0 6.3 multiply_reduce_fusion.5
  21.3 3.0 collective-permute-start.3
  33.7 2.7 collective-permute-start.9
  42.4 3.0 multiply_convert_fusion.5
  57.3 7.7 %multiply_reduce_fusion.4 = (f32[512]{0:T(512)S(1)}, f32[1536,512]{1,0:T(8,128)S(1)}) fusion(f32[1536]{0:T(1024)S(1)} %fusion.57, bf16[1536,4608]{1,0:T(8,128)(2,1)S(1)} %fusion.22, bf16[4608,512]{1,0:T(8,128)(2,1)S(1)} %bitcast.24), kind=kOutput, calls=%fused_computation.84 | convolution fusion | flops 7249329664 | bytes 22028288 | tf_op jit(solution)/shard_map/dot_general | solution.py:170
  81.1 2.5 collective-permute-done.14
  84.9 4.4 multiply_reduce_fusion.1
  90.6 3.0 fusion
  98.0 2.5 collective-permute-done.16
  113.0 2.8 collective-permute-done.19
  117.8 16.4 %fusion.94 = (f32[2048]{0:T(1024)S(1)}, f32[2048]{0:T(1024)S(1)}, f32[1536,2048]{1,0:T(8,128)}, bf16[1536,2048]{1,0:T(8,128)(2,1)}) fusion(f32[2048]{0:T(1024)S(1)} %get-tuple-element.77, f32[1536,2048]{1,0:T(8,128)S(1)} %get-tuple-element.164, f32[2048]{0:T(1024)S(1)} %get-tuple-element.47, bf16[1536,2048]{1,0:T(8,128)(2,1)} %param.28, f32[2048]{0:T(1024)} %param.38, ...), kind=kLoop, calls=%fused_computation.339 | loop fusion | flops 69201920 | bytes 44095488 | tf_op jit(solution)/shard_map/reduce_sum | solution.py:118
  137.1 2.5 collective-permute-done.21
  149.9 2.5 collective-permute-done.24
  153.1 8.4 %multiply_convert_fusion = bf16[1536,2048]{1,0:T(8,128)(2,1)S(1)} fusion(f32[1536,2048]{1,0:T(8,128)} %get-tuple-element.78, f32[1536,2048]{1,0:T(8,128)S(1)} %get-tuple-element.164, f32[]{:T(128)} %get-tuple-element.146, f32[2048]{0:T(1024)S(1)} %get-tuple-element.53, f32[2048]{0:T(1024)S(1)} %get-tuple-element.54, f32[2048]{0:T(1024)S(1)} %get-tuple-element.76, ...), kind=kLoop, calls=%fused_computation.3 | loop fusion | flops 28311552 | bytes 31504388 | tf_op jit(solution)/shard_map/convert_element_type | solution.py:185
  161.6 6.9 %fusion.96 = (f32[512]{0:T(512)S(1)}, f32[512]{0:T(512)S(1)}, f32[1536,512]{1,0:T(8,128)}) fusion(f32[512]{0:T(512)S(1)} %copy-done.29, f32[1536,512]{1,0:T(8,128)S(1)} %get-tuple-element.162, f32[512]{0:T(512)S(1)} %copy-done.33, f32[512]{0:T(512)S(1)} %copy-done.49, f32[512]{0:T(512)S(1)} %copy-done.46, f32[1536]{0:T(1024)S(1)} %fusion.57, ...), kind=kOutput, calls=%fused_computation.341 | convolution fusion | flops 3233807360 | bytes 14698496 | tf_op jit(solution)/shard_map/dot_general | solution.py:21
  186.0 4.4 multiply_convert_fusion.3
  190.4 10.5 %fusion.108 = f32[4608,512]{1,0:T(8,128)S(1)} fusion(bf16[1536,4608]{1,0:T(8,128)(2,1)} %copy-done.19, bf16[1536,512]{1,0:T(8,128)(2,1)S(1)} %multiply_convert_fusion.3), kind=kOutput, calls=%fused_computation.352 | convolution fusion | flops 7247757312 | bytes 25165824 | tf_op jit(solution)/shard_map/dot_general | solution.py:15
  200.9 3.0 constant_dynamic-slice_fusion.3
  207.7 15.1 %fusion.106 = f32[1536,4608]{1,0:T(8,128)} fusion(bf16[1536,512]{1,0:T(8,128)(2,1)S(1)} %multiply_convert_fusion.3, bf16[4608,512]{1,0:T(8,128)(2,1)} %param.31), kind=kOutput, calls=%fused_computation.350 | convolution fusion | flops 7247757312 | bytes 34603008 | tf_op jit(solution)/shard_map/dot_general | solution.py:21
  222.8 4.9 dynamic-slice_add_fusion
  230.8 16.6 %slice_multiply_fusion.8 = (f32[1536,512]{1,0:T(8,128)S(1)}, f32[1536,512]{1,0:T(8,128)S(1)}, f32[1536,512]{1,0:T(8,128)}, f32[1536,512]{1,0:T(8,128)}, f32[1536...) fusion(f32[1536,4608]{1,0:T(8,128)} %fusion.106, ...), kind=kLoop, calls=%fused_computation.75 | loop fusion | flops 6291456 | bytes 50380800 | tf_op jit(solution)/shard_map/mul | solution.py:198
  247.5 16.8 %fusion.95 = (f32[512]{0:T(512)S(1)}, f32[512]{0:T(512)S(1)}, f32[1536,512]{1,0:T(8,128)}) fusion(f32[512]{0:T(512)S(1)} %copy-done.21, f32[1536,512]{1,0:T(8,128)S(1)} %copy-done.4, f32[512]{0:T(512)S(1)} %copy-done.23, f32[512]{0:T(512)S(1)} %copy-done.27, f32[512]{0:T(512)S(1)} %copy-done.25, f32[1536]{0:T(1024)S(1)} %fusion.57, s32[]{:T(128)S(6)} %select_n.489, ...), kind=kLoop, calls=%fused_computation.340 | loop fusion | flops 25951232 | bytes 34627608 | tf_op jit(solution)/shard_map/reduce_sum | solution.py:118
  264.7 18.7 %collective-permute-done.46 = f32[1152,512]{1,0:T(8,128)} collective-permute-done((f32[1152,512]{1,0:T(8,128)}, f32[1152,512]{1,0:T(8,128)}, u32[]{:S(2)}, u32[]{:S(2)}) %collective-permute-start.46) | collective-permute-done | bytes 2359328 | tf_op jit(solution)/shard_map/ppermute | solution.py:61
  292.9 22.0 %collective-permute-done.32 = f32[4,512]{1,0:T(4,128)S(1)} collective-permute-done((f32[4,512]{1,0:T(4,128)S(1)}, f32[4,512]{1,0:T(4,128)S(1)}, u32[]{:S(2)}, u32[]{:S(2)}) %collective-permute-start.32) | collective-permute-done | bytes 8224 | tf_op jit(solution)/shard_map/ppermute | solution.py:61
  323.7 4.5 multiply_convert_fusion.2
  330.3 5.8 fusion.107
  343.0 13.3 %collective-permute-done.49 = f32[144,512]{1,0:T(8,128)S(1)} collective-permute-done((f32[144,512]{1,0:T(8,128)S(1)}, f32[144,512]{1,0:T(8,128)S(1)}, u32[]{:S(2)}, u32[]{:S(2)}) %collective-permute-start.49) | collective-permute-done | bytes 294944 | tf_op jit(solution)/shard_map/ppermute | solution.py:61
  356.4 14.5 %collective-permute-done.50 = f32[144,512]{1,0:T(8,128)S(1)} collective-permute-done((f32[144,512]{1,0:T(8,128)S(1)}, f32[144,512]{1,0:T(8,128)S(1)}, u32[]{:S(2)}, u32[]{:S(2)}) %collective-permute-start.50) | collective-permute-done | bytes 294944 | tf_op jit(solution)/shard_map/ppermute | solution.py:61
  371.8 2.8 bitcast_add_fusion
  376.7 10.6 %collective-permute-done.51 = f32[288,512]{1,0:T(8,128)S(1)} collective-permute-done((f32[288,512]{1,0:T(8,128)}, f32[288,512]{1,0:T(8,128)S(1)}, u32[]{:S(2)}, u32[]{:S(2)}) %collective-permute-start.51) | collective-permute-done | bytes 589856 | tf_op jit(solution)/shard_map/ppermute | solution.py:61
  390.0 11.1 %collective-permute-done.36 = f32[512,512]{0,1:T(8,128)} collective-permute-done((f32[512,512]{0,1:T(8,128)}, f32[512,512]{0,1:T(8,128)}, u32[]{:S(2)}, u32[]{:S(2)}) %collective-permute-start.36) | collective-permute-done | bytes 1048608 | tf_op jit(solution)/shard_map/ppermute | solution.py:61
  404.2 13.3 %collective-permute-done.52 = f32[576,512]{1,0:T(8,128)} collective-permute-done((f32[576,512]{1,0:T(8,128)S(1)}, f32[576,512]{1,0:T(8,128)}, u32[]{:S(2)}, u32[]{:S(2)}) %collective-permute-start.52) | collective-permute-done | bytes 1179680 | tf_op jit(solution)/shard_map/ppermute | solution.py:61
  421.6 5.2 collective-permute-done.37
  427.6 6.1 collective-permute-done.38
  435.5 10.9 %collective-permute-done.39 = f32[64,512]{0,1:T(8,128)S(1)} collective-permute-done((f32[64,512]{0,1:T(8,128)S(1)}, f32[64,512]{0,1:T(8,128)S(1)}, u32[]{:S(2)}, u32[]{:S(2)}) %collective-permute-start.39) | collective-permute-done | bytes 131104 | tf_op jit(solution)/shard_map/ppermute | solution.py:61
  446.5 13.2 %collective-permute-done.40 = f32[64,512]{0,1:T(8,128)S(1)} collective-permute-done((f32[64,512]{0,1:T(8,128)S(1)}, f32[64,512]{0,1:T(8,128)S(1)}, u32[]{:S(2)}, u32[]{:S(2)}) %collective-permute-start.40) | collective-permute-done | bytes 131104 | tf_op jit(solution)/shard_map/ppermute | solution.py:61
  460.0 8.2 %collective-permute-done.41 = f32[128,512]{0,1:T(8,128)S(1)} collective-permute-done((f32[128,512]{0,1:T(8,128)S(1)}, f32[128,512]{0,1:T(8,128)S(1)}, u32[]{:S(2)}, u32[]{:S(2)}) %collective-permute-start.41) | collective-permute-done | bytes 262176 | tf_op jit(solution)/shard_map/ppermute | solution.py:61
  473.0 2.8 pad_maximum_fusion.1
  477.5 4.1 collective-permute-done.42
  482.7 22.6 %collective-permute-done.43 = f32[512,512]{0,1:T(8,128)S(1)} collective-permute-done((f32[512,512]{0,1:T(8,128)S(1)}, f32[512,512]{0,1:T(8,128)S(1)}, u32[]{:S(2)}, u32[]{:S(2)}) %collective-permute-start.43) | collective-permute-done | bytes 1048608 | tf_op jit(solution)/shard_map/ppermute | solution.py:61
  508.2 5.6 fusion.92
  513.8 12.5 %add_convert_fusion = bf16[1536,2048]{1,0:T(8,128)(2,1)} fusion(f32[1536,2048]{1,0:T(8,128)} %get-tuple-element.78, bf16[1536,512]{1,0:T(8,128)(2,1)} %copy-done.18, bf16[2048,512]{1,0:T(8,128)(2,1)} %param.30), kind=kOutput, calls=%fused_computation.2 | convolution fusion | flops 3227516928 | bytes 22544384 | tf_op jit(solution)/shard_map/dot_general | solution.py:21
  528.3 2.5 pad_maximum_fusion.2
  530.9 5.4 copy.24
  536.3 7.2 %broadcast_select_fusion.1 = (f32[2304,512]{1,0:T(8,128)S(1)}, f32[2304,512]{1,0:T(8,128)}) fusion(f32[2304,512]{1,0:T(8,128)} %collective-permute-done.54, pred[]{:T(512)S(6)} %ne.465, f32[1152,512]{1,0:T(8,128)} %copy-done.6, f32[1152,512]{1,0:T(8,128)} %copy-done.5), kind=kLoop, calls=%fused_computation.93 | loop fusion | flops 3538944 | bytes 18874368 | tf_op jit(solution)/shard_map/jit(_where)/select_n | solution.py:99
  543.5 7.4 %pad_maximum_fusion = f32[4608,512]{1,0:T(8,128)} fusion(f32[2304,512]{1,0:T(8,128)} %get-tuple-element.103, f32[2304,512]{1,0:T(8,128)S(1)} %get-tuple-element.102), kind=kLoop, calls=%fused_computation.11 | loop fusion | flops 2359296 | bytes 18874368 | tf_op jit(solution)/shard_map/concatenate | solution.py:98
  550.8 103.5 %all-reduce.2.cloned.1.call-done = f32[512,2048]{1,0:T(8,128)} async-done(((f32[512,2048]{1,0:T(8,128)}), f32[512,2048]{1,0:T(8,128)}) %all-reduce.2.cloned.1.call-update) | async-done | bytes 4194320 | tf_op jit(solution)/shard_map/psum | solution.py:186
  654.3 4.8 copy.35
  (329 shorter events, 165.9 us)
Async XLA Ops:
  7.2 647.1 %all-reduce.2.cloned.1.call-start = ((), (), s32[]{:S(2)}) async-start(), calls=%async_computation | async-start | bytes 8388608 | tf_op jit(solution)/shard_map/psum | solution.py:186
  17.5 6.8 %collective-permute-start = (f32[4,512]{1,0:T(4,128)S(1)}, f32[4,512]{1,0:T(4,128)S(1)}, u32[]{:S(2)}, u32[]{:S(2)}) collective-permute-start(f32[4,512]{1,0:T(4,128)S(1)} %pad_maximum_fusion.18), channel_id=1, source_target_pairs={{0,1},{1,0},{2,3},{3,2},{4,5},{5,4},{6,7},{7,6},{8,9},{9,8},{10,11... | collective-permute-start | bytes 24584 | tf_op jit(solution)/shard_map/ppermute | solution.py:61
  21.3 4.5 collective-permute-start.3
  24.4 3.7 collective-permute-start.2
  25.8 3.9 collective-permute-start.5
  28.2 3.7 collective-permute-start.4
  29.8 3.8 collective-permute-start.7
  32.0 4.3 collective-permute-start.6
  33.7 4.8 collective-permute-start.9
  36.4 4.6 collective-permute-start.8
  67.6 3.7 collective-permute-start.11
  71.4 3.7 collective-permute-start.12
  75.2 3.7 collective-permute-start.13
  79.0 4.6 collective-permute-start.14
  96.5 4.0 collective-permute-start.16
  101.3 4.0 collective-permute-start.17
  106.1 4.0 collective-permute-start.18
  110.8 4.9 collective-permute-start.19
  135.6 4.0 collective-permute-start.21
  139.6 4.0 collective-permute-start.22
  143.6 4.0 collective-permute-start.23
  147.6 4.9 collective-permute-start.24
  169.8 3.7 collective-permute-start.26
  180.8 4.5 collective-permute-start.29
  206.0 16.8 %collective-permute-start.45 = (f32[2304,512]{1,0:T(8,128)}, f32[2304,512]{1,0:T(8,128)}, u32[]{:S(2)}, u32[]{:S(2)}) collective-permute-start(f32[2304,512]{1,0:T(8,128)} %constant_dynamic-slice_fusion.3), channel_id=1, source_target_pairs={{0,1},{1,0},{2,3},{3,2},{4,5},{5,4},{6,7},{7,6},{8,9},{9,8},{10,11... | collective-permute-start | bytes 14155784 | tf_op jit(solution)/shard_map/ppermute | solution.py:61
  229.4 54.0 %collective-permute-start.46 = (f32[1152,512]{1,0:T(8,128)}, f32[1152,512]{1,0:T(8,128)}, u32[]{:S(2)}, u32[]{:S(2)}) collective-permute-start(f32[1152,512]{1,0:T(8,128)} %constant_dynamic-slice_fusion.2), channel_id=1, source_target_pairs={{0,2},{1,3},{2,0},{3,1},{4,6},{5,7},{6,4},{7,5},{8,10},{9,11},{10,... | collective-permute-start | bytes 7077896 | tf_op jit(solution)/shard_map/ppermute | solution.py:61
  264.4 24.2 %collective-permute-start.30 = (f32[4,512]{1,0:T(4,128)S(1)}, f32[4,512]{1,0:T(4,128)S(1)}, u32[]{:S(2)}, u32[]{:S(2)}) collective-permute-start(f32[4,512]{1,0:T(4,128)S(1)} %pad_maximum_fusion.29), channel_id=1, source_target_pairs={{0,1},{1,0},{2,3},{3,2},{4,5},{5,4},{6,7},{7,6},{8,9},{9,8},{10,11... | collective-permute-start | bytes 24584 | tf_op jit(solution)/shard_map/ppermute | solution.py:61
  287.0 41.2 %collective-permute-start.47 = (f32[576,512]{1,0:T(8,128)S(1)}, f32[576,512]{1,0:T(8,128)S(1)}, u32[]{:S(2)}, u32[]{:S(2)}) collective-permute-start(f32[576,512]{1,0:T(8,128)S(1)} %constant_dynamic-slice_fusion.1), channel_id=1, source_target_pairs={{0,4},{1,5},{2,6},{3,7},{4,0},{5,1},{6,2},{7,3},{8,12},{9,13},{10,... | collective-permute-start | bytes 3538952 | tf_op jit(solution)/shard_map/ppermute | solution.py:61
  288.6 3.7 collective-permute-start.31
  292.4 22.5 %collective-permute-start.32 = (f32[4,512]{1,0:T(4,128)S(1)}, f32[4,512]{1,0:T(4,128)S(1)}, u32[]{:S(2)}, u32[]{:S(2)}) collective-permute-start(f32[4,512]{1,0:T(4,128)S(1)} %add.836), channel_id=1, source_target_pairs={{0,4},{1,5},{2,6},{3,7},{4,0},{5,1},{6,2},{7,3},{8,12},{9,13},{10,... | collective-permute-start | bytes 24584 | tf_op jit(solution)/shard_map/ppermute | solution.py:61
  318.5 4.5 collective-permute-start.34
  328.6 11.8 %collective-permute-start.48 = (f32[288,512]{1,0:T(8,128)S(1)}, f32[288,512]{1,0:T(8,128)S(1)}, u32[]{:S(2)}, u32[]{:S(2)}) collective-permute-start(f32[288,512]{1,0:T(8,128)S(1)} %constant_dynamic-slice_fusion), channel_id=1, source_target_pairs={{0,8},{1,9},{2,10},{3,11},{4,12},{5,13},{6,14},{7,15},{8,0},{9,1},... | collective-permute-start | bytes 1769480 | tf_op jit(solution)/shard_map/ppermute | solution.py:61
  339.6 32.2 %collective-permute-start.35 = (f32[1024,512]{0,1:T(8,128)}, f32[1024,512]{0,1:T(8,128)}, u32[]{:S(2)}, u32[]{:S(2)}) collective-permute-start(f32[1024,512]{0,1:T(8,128)} %dynamic-slice_bitcast_fusion), channel_id=1, source_target_pairs={{0,1},{1,0},{2,3},{3,2},{4,5},{5,4},{6,7},{7,6},{8,9},{9,8},{10,11... | collective-permute-start | bytes 6291464 | tf_op jit(solution)/shard_map/ppermute | solution.py:61
  340.5 15.7 %collective-permute-start.49 = (f32[144,512]{1,0:T(8,128)S(1)}, f32[144,512]{1,0:T(8,128)S(1)}, u32[]{:S(2)}, u32[]{:S(2)}) collective-permute-start(f32[144,512]{1,0:T(8,128)S(1)} %constant_dynamic-slice_fusion.8), channel_id=1, source_target_pairs={{0,16},{1,17},{2,18},{3,19},{4,20},{5,21},{6,22},{7,23},{8,24},{9,... | collective-permute-start | bytes 884744 | tf_op jit(solution)/shard_map/ppermute | solution.py:61
  356.3 14.6 %collective-permute-start.50 = (f32[144,512]{1,0:T(8,128)S(1)}, f32[144,512]{1,0:T(8,128)S(1)}, u32[]{:S(2)}, u32[]{:S(2)}) collective-permute-start(f32[144,512]{1,0:T(8,128)S(1)} %dynamic-slice_add_fusion.6), channel_id=1, source_target_pairs={{0,16},{1,17},{2,18},{3,19},{4,20},{5,21},{6,22},{7,23},{8,24},{9,... | collective-permute-start | bytes 884744 | tf_op jit(solution)/shard_map/ppermute | solution.py:61
  371.8 15.5 %collective-permute-start.51 = (f32[288,512]{1,0:T(8,128)}, f32[288,512]{1,0:T(8,128)S(1)}, u32[]{:S(2)}, u32[]{:S(2)}) collective-permute-start(f32[288,512]{1,0:T(8,128)} %pad_maximum_fusion.9), channel_id=1, source_target_pairs={{0,8},{1,9},{2,10},{3,11},{4,12},{5,13},{6,14},{7,15},{8,0},{9,1},... | collective-permute-start | bytes 1769480 | tf_op jit(solution)/shard_map/ppermute | solution.py:61
  375.7 25.4 %collective-permute-start.36 = (f32[512,512]{0,1:T(8,128)}, f32[512,512]{0,1:T(8,128)}, u32[]{:S(2)}, u32[]{:S(2)}) collective-permute-start(f32[512,512]{0,1:T(8,128)} %constant_dynamic-slice_fusion.7), channel_id=1, source_target_pairs={{0,2},{1,3},{2,0},{3,1},{4,6},{5,7},{6,4},{7,5},{8,10},{9,11},{10,... | collective-permute-start | bytes 3145736 | tf_op jit(solution)/shard_map/ppermute | solution.py:61
  388.5 29.0 %collective-permute-start.52 = (f32[576,512]{1,0:T(8,128)S(1)}, f32[576,512]{1,0:T(8,128)}, u32[]{:S(2)}, u32[]{:S(2)}) collective-permute-start(f32[576,512]{1,0:T(8,128)S(1)} %pad_maximum_fusion.7), channel_id=1, source_target_pairs={{0,4},{1,5},{2,6},{3,7},{4,0},{5,1},{6,2},{7,3},{8,12},{9,13},{10,... | collective-permute-start | bytes 3538952 | tf_op jit(solution)/shard_map/ppermute | solution.py:61
  402.6 24.3 %collective-permute-start.37 = (f32[256,512]{0,1:T(8,128)S(1)}, f32[256,512]{0,1:T(8,128)S(1)}, u32[]{:S(2)}, u32[]{:S(2)}) collective-permute-start(f32[256,512]{0,1:T(8,128)S(1)} %constant_dynamic-slice_fusion.6), channel_id=1, source_target_pairs={{0,4},{1,5},{2,6},{3,7},{4,0},{5,1},{6,2},{7,3},{8,12},{9,13},{10,... | collective-permute-start | bytes 1572872 | tf_op jit(solution)/shard_map/ppermute | solution.py:61
  420.6 50.1 %collective-permute-start.53 = (f32[1152,512]{1,0:T(8,128)}, f32[1152,512]{1,0:T(8,128)}, u32[]{:S(2)}, u32[]{:S(2)}) collective-permute-start(f32[1152,512]{1,0:T(8,128)} %pad_maximum_fusion.5), channel_id=1, source_target_pairs={{0,2},{1,3},{2,0},{3,1},{4,6},{5,7},{6,4},{7,5},{8,10},{9,11},{10,... | collective-permute-start | bytes 7077896 | tf_op jit(solution)/shard_map/ppermute | solution.py:61
  427.0 6.7 %collective-permute-start.38 = (f32[128,512]{0,1:T(8,128)S(1)}, f32[128,512]{0,1:T(8,128)S(1)}, u32[]{:S(2)}, u32[]{:S(2)}) collective-permute-start(f32[128,512]{0,1:T(8,128)S(1)} %constant_dynamic-slice_fusion.5), channel_id=1, source_target_pairs={{0,8},{1,9},{2,10},{3,11},{4,12},{5,13},{6,14},{7,15},{8,0},{9,1},... | collective-permute-start | bytes 786440 | tf_op jit(solution)/shard_map/ppermute | solution.py:61
  433.9 12.4 %collective-permute-start.39 = (f32[64,512]{0,1:T(8,128)S(1)}, f32[64,512]{0,1:T(8,128)S(1)}, u32[]{:S(2)}, u32[]{:S(2)}) collective-permute-start(f32[64,512]{0,1:T(8,128)S(1)} %constant_dynamic-slice_fusion.4), channel_id=1, source_target_pairs={{0,16},{1,17},{2,18},{3,19},{4,20},{5,21},{6,22},{7,23},{8,24},{9,... | collective-permute-start | bytes 393224 | tf_op jit(solution)/shard_map/ppermute | solution.py:61
  446.5 13.3 %collective-permute-start.40 = (f32[64,512]{0,1:T(8,128)S(1)}, f32[64,512]{0,1:T(8,128)S(1)}, u32[]{:S(2)}, u32[]{:S(2)}) collective-permute-start(f32[64,512]{0,1:T(8,128)S(1)} %dynamic-slice_add_fusion.7), channel_id=1, source_target_pairs={{0,16},{1,17},{2,18},{3,19},{4,20},{5,21},{6,22},{7,23},{8,24},{9,... | collective-permute-start | bytes 393224 | tf_op jit(solution)/shard_map/ppermute | solution.py:61
  459.9 8.3 %collective-permute-start.41 = (f32[128,512]{0,1:T(8,128)S(1)}, f32[128,512]{0,1:T(8,128)S(1)}, u32[]{:S(2)}, u32[]{:S(2)}) collective-permute-start(f32[128,512]{0,1:T(8,128)S(1)} %pad_maximum_fusion.11), channel_id=1, source_target_pairs={{0,8},{1,9},{2,10},{3,11},{4,12},{5,13},{6,14},{7,15},{8,0},{9,1},... | collective-permute-start | bytes 786440 | tf_op jit(solution)/shard_map/ppermute | solution.py:61
  468.4 13.2 %collective-permute-start.42 = (f32[256,512]{0,1:T(8,128)S(1)}, f32[256,512]{0,1:T(8,128)S(1)}, u32[]{:S(2)}, u32[]{:S(2)}) collective-permute-start(f32[256,512]{0,1:T(8,128)S(1)} %pad_maximum_fusion.10), channel_id=1, source_target_pairs={{0,4},{1,5},{2,6},{3,7},{4,0},{5,1},{6,2},{7,3},{8,12},{9,13},{10,... | collective-permute-start | bytes 1572872 | tf_op jit(solution)/shard_map/ppermute | solution.py:61
  477.5 58.8 %collective-permute-start.54 = (f32[2304,512]{1,0:T(8,128)}, f32[2304,512]{1,0:T(8,128)}, u32[]{:S(2)}, u32[]{:S(2)}) collective-permute-start(f32[2304,512]{1,0:T(8,128)} %pad_maximum_fusion.1), channel_id=1, source_target_pairs={{0,1},{1,0},{2,3},{3,2},{4,5},{5,4},{6,7},{7,6},{8,9},{9,8},{10,11... | collective-permute-start | bytes 14155784 | tf_op jit(solution)/shard_map/ppermute | solution.py:61
  481.8 23.5 %collective-permute-start.43 = (f32[512,512]{0,1:T(8,128)S(1)}, f32[512,512]{0,1:T(8,128)S(1)}, u32[]{:S(2)}, u32[]{:S(2)}) collective-permute-start(f32[512,512]{0,1:T(8,128)S(1)} %pad_maximum_fusion.8), channel_id=1, source_target_pairs={{0,2},{1,3},{2,0},{3,1},{4,6},{5,7},{6,4},{7,5},{8,10},{9,11},{10,... | collective-permute-start | bytes 3145736 | tf_op jit(solution)/shard_map/ppermute | solution.py:61
  507.1 19.2 %collective-permute-start.44 = (f32[1024,512]{0,1:T(8,128)}, f32[1024,512]{0,1:T(8,128)}, u32[]{:S(2)}, u32[]{:S(2)}) collective-permute-start(f32[1024,512]{0,1:T(8,128)} %pad_maximum_fusion.6), channel_id=1, source_target_pairs={{0,1},{1,0},{2,3},{3,2},{4,5},{5,4},{6,7},{7,6},{8,9},{9,8},{10,11... | collective-permute-start | bytes 6291464 | tf_op jit(solution)/shard_map/ppermute | solution.py:61
  (63 other events, 1138.0 us)
Sparse Core Ops, SparseCore 0:
  513.9 140.3 all-reduce.1

commit v2 on v0

v2 whole, which is shorter than its diff:
```python
import functools

import jax
import jax.numpy as jnp
from jax import lax
from jax.experimental import pallas as pl
from jax.experimental.pallas import tpu as pltpu
from jax.sharding import PartitionSpec as P

epsilon = 1e-05
pad = 8
lane = 256
shared = 2
ragged = 64
VM = pl.BlockSpec(memory_space=pltpu.VMEM)
SM = pl.BlockSpec(memory_space=pltpu.SMEM)
ANY = pl.BlockSpec(memory_space=pl.ANY)
HBM = pl.BlockSpec(memory_space=pltpu.HBM)
OFFSETS = [(r, c) for r in (-1, 0, 1) for c in (-1, 0, 1)]


def params(mib):
    return pltpu.CompilerParams(vmem_limit_bytes=mib * 1024 * 1024)


def cost(flops, moved):
    return pl.CostEstimate(flops=int(flops), bytes_accessed=int(moved), transcendentals=0)


def struct(shape, dtype=jnp.float32):
    return jax.ShapeDtypeStruct(shape, dtype)


def dot(left, right):
    return jnp.dot(left, right, preferred_element_type=jnp.float32)


def dot_cols(left, right):
    return lax.dot_general(
        left, right, (((1,), (1,)), ((), ())), preferred_element_type=jnp.float32
    )


def dot_rows(left, right):
    return lax.dot_general(
        left, right, (((0,), (0,)), ((), ())), preferred_element_type=jnp.float32
    )


def sigmoid(v):
    return 0.5 * jnp.tanh(0.5 * v) + 0.5


def slope_of(act):
    sig = sigmoid(act)
    value = act * sig
    return sig + value * (1.0 - sig)


def row_ids(start, rows, width):
    return lax.broadcasted_iota(jnp.int32, (rows, width), 0) + start


def fill(values, filled, start=0, total=None):
    rows, width = values.shape
    total = rows if total is None else total
    safe = max(0, min(rows, total - ragged - start))
    if safe == rows:
        return values
    rest = jnp.where(row_ids(start + safe, rows - safe, width) < filled, values[safe:], 0.0)
    return rest if safe == 0 else jnp.concatenate([values[:safe], rest], axis=0)


def column_sum(values):
    return jnp.sum(values, axis=0, keepdims=True)


def moments(values, filled, count):
    mean = column_sum(fill(values, filled)) / count
    gap = fill(values - mean, filled)
    return mean, column_sum(gap * gap)


def put_rows(packed, stream, at, row):
    packed[at : at + 1, :] = jnp.where(stream == 0, row, 0.0)
    packed[at + 1 : at + 2, :] = jnp.where(stream == 0, 0.0, row)


def pick(table, stream, at):
    return jnp.where(stream == 0, table[at : at + 1, :], table[at + 1 : at + 2, :])


def pair_up(tables, join):
    tables = list(tables)
    while len(tables) > 1:
        tables = [join(tables[k], tables[k + 1]) for k in range(0, len(tables), 2)]
    return tables[0]


def join_moments(left, right):
    mean, square, count = left
    other_mean, other_square, other_count = right
    number = count + other_count
    share = other_count / jnp.maximum(number, 1.0)
    gap = other_mean - mean
    return (
        mean + gap * share,
        square + other_square + gap * gap * (count * share),
        number,
    )


def merge_norm(tables, tallies, stream):
    mean, square, number = pair_up(
        [
            (pick(table, stream, 0), pick(table, stream, 2), pick(tally, stream, 4))
            for table, tally in zip(tables, tallies)
        ],
        join_moments,
    )
    return mean, lax.rsqrt(square / number + epsilon), number


def sum_tables(tables, stream, at):
    return pair_up([pick(table, stream, at) for table in tables], lambda a, b: a + b)


def first_kernel(ints, features, reducer, pre, packed, held, weights, sems):
    rows, depth = features.shape
    pieces = held.shape[0] // (held.shape[0] // (sems.shape[0] - 1))
    tile = rows // pieces
    load = pltpu.make_async_copy(reducer, weights, sems.at[pieces])
    load.start()
    copies = []
    for k in range(pieces):
        at = pl.ds(k * tile, tile)
        copies.append(pltpu.make_async_copy(features.at[at, :], held.at[at, :], sems.at[k]))
    for copy in copies:
        copy.start()
    load.wait()
    filled, stream = ints[1], ints[2]
    parts = []

    def settle(k):
        values = pre[k * tile : (k + 1) * tile, :]
        count = jnp.minimum(filled - k * tile, tile).astype(jnp.float32)
        mean = column_sum(fill(values, filled, k * tile, rows)) / count
        gap = fill(values - mean, filled, k * tile, rows)
        parts.append((mean, column_sum(gap * gap), jnp.full_like(mean, count)))

    for k in range(pieces):
        copies[k].wait()
        at = slice(k * tile, (k + 1) * tile)
        pre[at, :] = dot(held[at, :], weights[...])
        if k:
            settle(k - 1)
    settle(pieces - 1)
    mean, square, count = functools.reduce(join_moments, parts)
    put_rows(packed, stream, 0, mean)
    put_rows(packed, stream, 2, square)
    put_rows(packed, stream, 4, count)
    packed[6:8, :] = jnp.zeros((2, mean.shape[1]), jnp.float32)


def first_stage(ints, features, reducer, pieces=3):
    rows, depth = features.shape
    width = reducer.shape[1]
    return pl.pallas_call(
        first_kernel,
        in_specs=[SM, ANY, ANY],
        out_specs=[VM, VM],
        out_shape=[struct((rows, width)), struct((8, width))],
        scratch_shapes=[
            pltpu.VMEM((rows, depth), jnp.bfloat16),
            pltpu.VMEM((depth, width), jnp.bfloat16),
            pltpu.SemaphoreType.DMA((pieces + 1,)),
        ],
        compiler_params=params(50),
        cost_estimate=cost(2 * rows * depth * width, 12e6),
        name="first_stage",
    )(ints, features, reducer)


def place(start, rows, side):
    rows_f = (row_ids(start, rows, 128)).astype(jnp.float32) + 0.5
    side_f = side.astype(jnp.float32)
    area_f = side_f * side_f
    within = rows_f - jnp.floor(rows_f / area_f) * area_f
    high = jnp.floor(within / side_f)
    across = jnp.floor(within - high * side_f)
    return high, across


def inside(high, across, side, delta_row, delta_col):
    last = side.astype(jnp.float32) - 1.0
    parts = []
    if delta_row < 0:
        parts.append(high > 0.0)
    if delta_row > 0:
        parts.append(high < last)
    if delta_col < 0:
        parts.append(across > 0.0)
    if delta_col > 0:
        parts.append(across < last)
    keep = parts[0]
    for part in parts[1:]:
        keep = keep & part
    return keep


def spread(mask, width):
    return jnp.concatenate([mask] * (width // 128), axis=1)


def moved(held, start, rows):
    width = held.shape[1]
    base = pl.multiple_of((start // 8) * 8, 8)
    extra = start - base
    tiles = held[pl.ds(base, rows + 8), :].reshape(rows // 8 + 1, 8, width)
    tiles = pltpu.roll(tiles, lax.rem(8 - extra, 8), axis=1)
    first = lax.broadcasted_iota(jnp.int32, (1, 8, width), 1) < 8 - extra
    return jnp.where(first, tiles[:-1], tiles[1:]).reshape(rows, width)


def hold(held, values, rows):
    held[0:pad, :] = jnp.zeros((pad, held.shape[1]), jnp.float32)
    held[pad + rows :, :] = jnp.zeros((2 * pad, held.shape[1]), jnp.float32)
    held[pad : pad + rows, :] = values.astype(jnp.bfloat16).astype(jnp.float32)


def keep_norm(norm, mean, inverse, gain, bias, number):
    norm[0:1, :] = mean
    norm[1:2, :] = inverse
    norm[2:3, :] = gain
    norm[3:4, :] = bias
    norm[4:5, :] = number
    norm[5:8, :] = jnp.zeros((3, mean.shape[1]), jnp.float32)


def stream_weights(spatial, weights, sems):
    rows = spatial.shape[0] // 3
    copies = []
    for k in range(3):
        at = pl.ds(k * rows, rows)
        copies.append(pltpu.make_async_copy(spatial.at[at, :], weights.at[at, :], sems.at[k]))
        copies[k].start()
    return copies


def middle_kernel(ints, *refs):
    tables, refs = refs[:-11], refs[-11:]
    gain, bias, pre, spatial, low, out, packed, norm, held, weights, sems = refs
    side, filled, stream = ints[0], ints[1], ints[2]
    rows, width = pre.shape
    copies = stream_weights(spatial, weights, sems)
    mean, inverse, number = merge_norm(tables, tables, stream)
    keep_norm(norm, mean, inverse, gain[...], bias[...], number)
    act = (pre[...] - mean) * (inverse * gain[...]) + bias[...]
    value = fill(act * sigmoid(act), filled)
    low[...] = value.astype(jnp.bfloat16)
    hold(held, value, rows)
    high, across = place(0, rows, side)
    total = jnp.zeros((rows, width), jnp.float32)
    for tap, (dr, dc) in enumerate(OFFSETS):
        piece = moved(held, pad + dr * side + dc, rows)
        if (dr, dc) != (0, 0):
            piece = jnp.where(spread(inside(high, across, side, dr, dc), width), piece, 0.0)
        if tap % 3 == 0:
            copies[tap // 3].wait()
        total += dot(piece.astype(jnp.bfloat16), weights[tap * width : (tap + 1) * width, :])
    out[...] = total
    mean, square = moments(out[...], filled, filled.astype(jnp.float32))
    put_rows(packed, stream, 0, mean)
    put_rows(packed, stream, 2, square)


def middle_stage(ints, tables, gain, bias, pre, spatial):
    rows, width = pre.shape
    return pl.pallas_call(
        middle_kernel,
        in_specs=[SM] + [VM] * (len(tables) + 3) + [HBM],
        out_specs=[VM, VM, VM, VM],
        out_shape=[
            struct((rows, width), jnp.bfloat16),
            struct((rows, width)),
            struct((4, width)),
            struct((8, width)),
        ],
        scratch_shapes=[
            pltpu.VMEM((rows + 3 * pad, width), jnp.float32),
            pltpu.VMEM(spatial.shape, jnp.bfloat16),
            pltpu.SemaphoreType.DMA((3,)),
        ],
        compiler_params=params(40),
        cost_estimate=cost(18 * rows * width * width, 12e6),
        name="middle_stage",
    )(ints, *tables, gain, bias, pre, spatial)


def last_kernel(ints, *refs):
    tables, refs = refs[:-7], refs[-7:]
    tables, tallies = tables[: len(tables) // 2], tables[len(tables) // 2 :]
    gain, bias, pre, expander, low, packed, norm = refs
    filled, stream = ints[1], ints[2]
    rows, width = pre.shape
    wide = expander.shape[1]
    mean, inverse, number = merge_norm(tables, tallies, stream)
    keep_norm(norm, mean, inverse, gain[...], bias[...], number)
    act = (pre[...] - mean) * (inverse * gain[...]) + bias[...]
    low[...] = fill(act * sigmoid(act), filled).astype(jnp.bfloat16)
    count = filled.astype(jnp.float32)
    for k in range(wide // width):
        at = slice(k * width, (k + 1) * width)
        mean, square = moments(dot(low[...], expander[:, at]), filled, count)
        put_rows(packed.at[:, at], stream, 0, mean)
        put_rows(packed.at[:, at], stream, 2, square)


def last_stage(ints, tables, tallies, gain, bias, pre, expander):
    rows, width = pre.shape
    wide = expander.shape[1]
    return pl.pallas_call(
        last_kernel,
        in_specs=[SM] + [VM] * (2 * len(tables) + 4),
        out_specs=[VM, VM, VM],
        out_shape=[
            struct((rows, width), jnp.bfloat16),
            struct((4, wide)),
            struct((8, width)),
        ],
        compiler_params=params(34),
        cost_estimate=cost(2 * rows * width * wide, 8e6),
        name="last_stage",
    )(ints, *tables, *tallies, gain, bias, pre, expander)


def head_kernel(ints, *refs):
    tables, refs = refs[:-13], refs[-13:]
    tables, tallies = tables[: len(tables) // 2], tables[len(tables) // 2 :]
    gain, bias, low, expander, features, upstream = refs[:6]
    out, grad, part, packed, norm, hat, raw = refs[6:]
    filled, stream = ints[1], ints[2]
    rows, width = low.shape
    tile = expander.shape[1]
    chunk = 384
    count = filled.astype(jnp.float32)
    mean, inverse, number = merge_norm(tables, tallies, stream)
    keep_norm(norm, mean, inverse, gain[...], bias[...], number)
    hat[...] = dot(low[...], expander[...])
    scale = 0.5 * gain[...] * inverse
    offset = 0.5 * bias[...] - mean * scale
    zero = jnp.zeros((8, tile), jnp.float32)

    def body(k, sums, masked):
        at = pl.ds(pl.multiple_of(k * chunk, chunk), chunk)
        pre = hat[at, :]
        near = features[at, :] * jnp.bfloat16(0.5)
        half = pre * scale + offset + near.astype(jnp.float32)
        bent = jnp.tanh(half)
        up = 1.0 + bent
        value = half * up
        g = upstream[at, :].astype(jnp.float32) * (up + value * (1.0 - bent))
        if masked:
            used = row_ids(k * chunk, chunk, tile) < filled
            value = jnp.where(used, value, 0.0)
            g = jnp.where(used, g, 0.0)
        out[at, :] = value.astype(jnp.bfloat16)
        raw[at, :] = g
        grad[at, :] = g.astype(jnp.bfloat16)
        return (
            sums[0] + jnp.sum(g.reshape(chunk // 8, 8, tile), axis=0),
            sums[1] + jnp.sum((g * pre).reshape(chunk // 8, 8, tile), axis=0),
        )

    last = rows // chunk - 1
    sums = lax.fori_loop(0, last, lambda k, sums: body(k, sums, False), (zero, zero))
    sums = body(last, sums, True)
    first = column_sum(sums[0])
    second = inverse * (column_sum(sums[1]) - mean * first)
    put_rows(packed, stream, 0, 0.5 * first)
    put_rows(packed, stream, 2, 0.5 * second)
    tilt = scale * inverse * second / count
    level = scale * first / count - mean * tilt

    def centre(k, start, masked):
        at = pl.ds(start, chunk)
        value = raw[at, :] * scale - hat[at, :] * tilt - level
        if masked:
            value = jnp.where(row_ids(start, chunk, tile) < filled, value, 0.0)
        part[at, :] = value.astype(jnp.bfloat16)
        return k

    lax.fori_loop(0, last, lambda k, _: centre(0, pl.multiple_of(k * chunk, chunk), False), 0)
    centre(0, last * chunk, True)


def head_stage(ints, tables, tallies, gain, bias, low, expander, features, upstream, tiles=4):
    rows, width = low.shape
    wide = expander.shape[1]
    tile = wide // tiles
    col = lambda i: (0, i)
    fix = lambda i: (0, 0)
    return pl.pallas_call(
        head_kernel,
        grid=(tiles,),
        in_specs=[
            SM,
            *([pl.BlockSpec((4, tile), col)] * len(tables)),
            *([pl.BlockSpec((8, tile), fix)] * len(tables)),
            pl.BlockSpec((1, tile), col),
            pl.BlockSpec((1, tile), col),
            pl.BlockSpec((rows, width), fix),
            pl.BlockSpec((width, tile), col),
            pl.BlockSpec((rows, tile), col),
            pl.BlockSpec((rows, tile), col),
        ],
        out_specs=[
            pl.BlockSpec((rows, tile), col),
            pl.BlockSpec((rows, tile), col),
            pl.BlockSpec((rows, tile), col),
            pl.BlockSpec((4, tile), col),
            pl.BlockSpec((8, tile), col),
        ],
        out_shape=[
            struct((rows, wide), jnp.bfloat16),
            struct((rows, wide), jnp.bfloat16),
            struct((rows, wide), jnp.bfloat16),
            struct((4, wide)),
            struct((8, wide)),
        ],
        scratch_shapes=[
            pltpu.VMEM((rows, tile), jnp.float32),
            pltpu.VMEM((rows, tile), jnp.float32),
        ],
        compiler_params=params(42),
        cost_estimate=cost(2 * rows * width * wide, 32e6),
        name="head_stage",
    )(ints, *tables, *tallies, gain, bias, low, expander, features, upstream)


def cov_kernel(ints, low, centred, cov):
    filled = ints[1]
    values = low[...].astype(jnp.float32)
    centre = column_sum(values) / filled.astype(jnp.float32)
    centred[...] = fill(values - centre, filled).astype(jnp.bfloat16)
    cov[...] = dot_rows(centred[...], centred[...]).astype(jnp.bfloat16)


def cov_stage(ints, low):
    rows, width = low.shape
    return pl.pallas_call(
        cov_kernel,
        in_specs=[SM, VM],
        out_specs=[VM, VM],
        out_shape=[struct((rows, width), jnp.bfloat16), struct((width, width), jnp.bfloat16)],
        compiler_params=params(20),
        cost_estimate=cost(2 * rows * width * width, 5e6),
        name="cov_stage",
    )(ints, low)


def weight_kernel(low, part, out):
    out[...] = dot_rows(low[...], part[...])


def weight_stage(low, part, place, places):
    rows, width = low.shape
    tile = part.shape[1] // places
    return pl.pallas_call(
        weight_kernel,
        grid=(1,),
        in_specs=[
            pl.BlockSpec((rows, width), lambda i: (0, 0)),
            pl.BlockSpec((rows, tile), lambda i: (0, place)),
        ],
        out_specs=pl.BlockSpec((width, tile), lambda i: (0, 0)),
        out_shape=struct((width, tile)),
        compiler_params=params(28),
        cost_estimate=cost(2 * rows * width * tile, 8e6),
        name="weight_stage",
    )(low, part)


def back_kernel(part, expander, out):
    out[...] = dot_cols(part[...], expander[...])


def back_stage(part, expander, place, places):
    rows, wide = part.shape
    width = expander.shape[0]
    tile = rows // places
    return pl.pallas_call(
        back_kernel,
        grid=(1,),
        in_specs=[
            pl.BlockSpec((tile, wide), lambda i: (place, 0)),
            pl.BlockSpec((width, wide), lambda i: (0, 0)),
        ],
        out_specs=pl.BlockSpec((tile, width), lambda i: (0, 0)),
        out_shape=struct((tile, width)),
        compiler_params=params(28),
        cost_estimate=cost(2 * tile * width * wide, 8e6),
        name="back_stage",
    )(part, expander)


def split_pair(row):
    high = row.astype(jnp.bfloat16)
    return high, (row - high.astype(jnp.float32)).astype(jnp.bfloat16)


def turn_kernel(ints, *refs):
    tables, refs = refs[:-14], refs[-14:]
    local, local_moments, norm_last, expander, centred, upper, lower, pre, norm = refs[:9]
    grad, packed, scaled, shift, eight = refs[9:]
    filled, stream = ints[1], ints[2]
    rows, width = pre.shape
    count = filled.astype(jnp.float32)
    mean, inverse, gain = norm_last[0:1, :], norm_last[1:2, :], norm_last[2:3, :]
    number = norm_last[4:5, :]
    scale = gain * inverse
    first = sum_tables(tables, stream, 0)
    second = sum_tables(tables, stream, 2)
    off_first = scale * (first / number - pick(local, stream, 0) / count)
    off_second = inverse * scale * (second / number - pick(local, stream, 2) / count)
    line = off_first + (pick(local_moments, stream, 0) - mean) * off_second
    shift[...] = line
    scaled[...] = (expander[...].astype(jnp.float32) * off_second).astype(jnp.bfloat16)
    square = dot_cols(scaled[...], expander[...]).astype(jnp.bfloat16)
    high, rest = split_pair(line)
    eight[...] = jnp.zeros_like(eight)
    eight[0:1, :] = high.astype(jnp.float32)
    eight[1:2, :] = rest.astype(jnp.float32)
    flat = column_sum(dot_cols(eight[...].astype(jnp.bfloat16), expander[...]))
    half = rows // 2
    chunk = half // 2
    sums = []
    for k in range(rows // chunk):
        at = slice(k * chunk, (k + 1) * chunk)
        source = upper if k * chunk < half else lower
        back = source[k * chunk % half : k * chunk % half + chunk, :]
        normed = (pre[at, :] - norm[0:1, :]) * norm[1:2, :]
        slope = slope_of(normed * norm[2:3, :] + norm[3:4, :])
        value = (back - dot(centred[at, :], square) - flat) * slope
        value = fill(value, filled, k * chunk, rows)
        grad[at, :] = value
        sums.append((column_sum(value), column_sum(value * normed)))
    put_rows(packed, stream, 0, sum(first for first, _ in sums))
    put_rows(packed, stream, 2, sum(second for _, second in sums))


def turn_stage(
    ints, tables, local, local_moments, norm_last, expander, centred, upper, lower, pre, norm
):
    rows, width = pre.shape
    wide = expander.shape[1]
    return pl.pallas_call(
        turn_kernel,
        in_specs=[SM] + [VM] * (len(tables) + 9),
        out_specs=[VM] * 4,
        out_shape=[
            struct((rows, width)),
            struct((4, width)),
            struct((width, wide), jnp.bfloat16),
            struct((1, wide)),
        ],
        scratch_shapes=[pltpu.VMEM((8, wide), jnp.float32)],
        compiler_params=params(30),
        cost_estimate=cost(4 * width * width * wide, 12e6),
        name="turn_stage",
    )(
        ints, *tables, local, local_moments, norm_last, expander, centred, upper, lower, pre, norm
    )


def mend_kernel(ints, left_weight, right_weight, cov, scaled, shift, low, send, kept, left, right):
    sums = column_sum(low[...].astype(jnp.float32))
    sums_high, sums_rest = split_pair(sums)
    line_high, line_rest = split_pair(shift[...])
    left[...] = jnp.zeros_like(left)
    right[...] = jnp.zeros_like(right)
    for at, a, b in (
        (0, sums_high, line_high),
        (1, sums_rest, line_high),
        (2, sums_high, line_rest),
    ):
        left[at : at + 1, :] = a.astype(jnp.float32)
        right[at : at + 1, :] = b.astype(jnp.float32)
    lower = ints[3] == 0
    width = low.shape[1]

    def block(weight, at, place):
        outer = dot_rows(left[...].astype(jnp.bfloat16), right[:, place].astype(jnp.bfloat16))
        return weight[:, at] - dot(cov[...], scaled[:, place]) - outer

    for k in range(send.shape[0] // width):
        at = slice(k * lane, (k + 1) * lane)
        rows = slice(k * width, (k + 1) * width)
        shift_by = scaled.shape[1] // 2
        first = block(left_weight, at, at)
        second = block(right_weight, at, slice(shift_by + k * lane, shift_by + (k + 1) * lane))
        send[rows, :] = jnp.where(lower, second, first)
        kept[rows, :] = jnp.where(lower, first, second)


def mend_stage(ints, left_weight, right_weight, cov, scaled, shift, low):
    width, wide = scaled.shape
    return pl.pallas_call(
        mend_kernel,
        in_specs=[SM] + [VM] * 6,
        out_specs=[VM, VM],
        out_shape=[struct((width * wide // (2 * lane), lane))] * 2,
        scratch_shapes=[
            pltpu.VMEM((16, width), jnp.float32),
            pltpu.VMEM((16, wide), jnp.float32),
        ],
        compiler_params=params(32),
        cost_estimate=cost(2 * width * width * wide, 14e6),
        name="mend_stage",
    )(ints, left_weight, right_weight, cov, scaled, shift, low)


def norm_grad(grad, pre, norm, tables, stream):
    scale = norm[2:3, :] * norm[1:2, :]
    first = sum_tables(tables, stream, 0) / norm[4:5, :]
    second = sum_tables(tables, stream, 2) / norm[4:5, :]
    normed = (pre[...] - norm[0:1, :]) * norm[1:2, :]
    return scale * (grad[...] - first - normed * second)


def halves(product, core):
    half = product.shape[1] // 2
    left, right = product[:, :half], product[:, half:]
    return jnp.where(core == 0, right, left), jnp.where(core == 0, left, right)


def turned_kernel(low, turned):
    turned[...] = low[...].T


def turned_stage(low):
    rows, width = low.shape
    return pl.pallas_call(
        turned_kernel,
        in_specs=[VM],
        out_specs=VM,
        out_shape=struct((width, rows), low.dtype),
        compiler_params=params(16),
        cost_estimate=cost(0, 2e6),
        name="turned_stage",
    )(low)


def taps_kernel(ints, *refs):
    tables, refs = refs[:-11], refs[-11:]
    grad, pre, norm, turned, rounded, send, kept, weight, held, slots, sems = refs
    side, filled, stream = ints[0], ints[1], ints[2]
    rows, width = grad.shape
    value = fill(norm_grad(grad, pre, norm, tables, stream), filled)
    rounded[...] = value.astype(jnp.bfloat16)
    hold(held, value, rows)
    high, across = place(0, rows, side)
    copies = []
    for tap, (dr, dc) in enumerate(OFFSETS):
        piece = moved(held, pad - dr * side - dc, rows)
        if (dr, dc) != (0, 0):
            piece = jnp.where(spread(inside(high, across, side, -dr, -dc), width), piece, 0.0)
        product = dot(turned[...], piece.astype(jnp.bfloat16))
        if tap < shared:
            at = slice(tap * width, (tap + 1) * width)
            send[at, :], kept[at, :] = halves(product, ints[3])
            continue
        k = tap - shared
        if k >= 3:
            copies[k - 3].wait()
        slots[k % 3] = product
        at = pl.ds(k * width, width)
        copies.append(pltpu.make_async_copy(slots.at[k % 3], weight.at[at, :], sems.at[k % 3]))
        copies[k].start()
    for copy in copies[-3:]:
        copy.wait()


def taps_stage(ints, tables, grad, pre, norm, turned):
    rows, width = grad.shape
    return pl.pallas_call(
        taps_kernel,
        in_specs=[SM] + [VM] * (len(tables) + 4),
        out_specs=[VM, VM, VM, HBM],
        out_shape=[
            struct((rows, width), jnp.bfloat16),
            struct((shared * width, lane)),
            struct((shared * width, lane)),
            struct(((9 - shared) * width, width)),
        ],
        scratch_shapes=[
            pltpu.VMEM((rows + 3 * pad, width), jnp.float32),
            pltpu.VMEM((3, width, width), jnp.float32),
            pltpu.SemaphoreType.DMA((3,)),
        ],
        compiler_params=params(44),
        cost_estimate=cost(18 * rows * width * width, 18e6),
        name="taps_stage",
    )(ints, *tables, grad, pre, norm, turned)


def down_kernel(ints, rounded, pre, norm, spatial, grad, packed, held, weights, sems):
    side, filled, stream = ints[0], ints[1], ints[2]
    rows, width = pre.shape
    copies = stream_weights(spatial, weights, sems)
    hold(held, rounded[...].astype(jnp.float32), rows)
    high, across = place(0, rows, side)
    total = jnp.zeros((rows, width), jnp.float32)
    for tap, (dr, dc) in enumerate(OFFSETS):
        piece = moved(held, pad - dr * side - dc, rows)
        if (dr, dc) != (0, 0):
            piece = jnp.where(spread(inside(high, across, side, -dr, -dc), width), piece, 0.0)
        if tap % 3 == 0:
            copies[tap // 3].wait()
        total += dot_cols(piece.astype(jnp.bfloat16), weights[tap * width : (tap + 1) * width, :])
    grad[...] = total
    normed = (pre[...] - norm[0:1, :]) * norm[1:2, :]
    act = normed * norm[2:3, :] + norm[3:4, :]
    value = fill(grad[...] * slope_of(act), filled)
    grad[...] = value
    put_rows(packed, stream, 0, column_sum(value))
    put_rows(packed, stream, 2, column_sum(value * normed))


def down_stage(ints, rounded, spatial, pre, norm):
    rows, width = pre.shape
    return pl.pallas_call(
        down_kernel,
        in_specs=[SM] + [VM] * 3 + [HBM],
        out_specs=[VM, VM],
        out_shape=[struct((rows, width)), struct((4, width))],
        scratch_shapes=[
            pltpu.VMEM((rows + 3 * pad, width), jnp.float32),
            pltpu.VMEM(spatial.shape, jnp.bfloat16),
            pltpu.SemaphoreType.DMA((3,)),
        ],
        compiler_params=params(40),
        cost_estimate=cost(18 * rows * width * width, 14e6),
        name="down_stage",
    )(ints, rounded, pre, norm, spatial)


def root_kernel(ints, *refs):
    tables, refs = refs[:-7], refs[-7:]
    grad, pre, norm, features, low, send, kept = refs
    filled, stream, core = ints[1], ints[2], ints[3]

    @pl.when(pl.program_id(0) == 0)
    def _():
        value = fill(norm_grad(grad, pre, norm, tables, stream), filled)
        low[...] = value.astype(jnp.bfloat16)

    send[...], kept[...] = halves(dot_rows(features[...], low[...]), core)


def root_stage(ints, tables, grad, pre, norm, features, tiles=4):
    rows, width = grad.shape
    wide = features.shape[1]
    tile = wide // tiles
    fix = lambda i: (0, 0)
    return pl.pallas_call(
        root_kernel,
        grid=(tiles,),
        in_specs=[
            SM,
            *([pl.BlockSpec((4, width), fix)] * len(tables)),
            pl.BlockSpec((rows, width), fix),
            pl.BlockSpec((rows, width), fix),
            pl.BlockSpec((8, width), fix),
            pl.BlockSpec((rows, tile), lambda i: (0, i)),
        ],
        out_specs=[
            pl.BlockSpec((rows, width), fix),
            pl.BlockSpec((tile, width // 2), lambda i: (i, 0)),
            pl.BlockSpec((tile, width // 2), lambda i: (i, 0)),
        ],
        out_shape=[
            struct((rows, width), jnp.bfloat16),
            struct((wide, width // 2)),
            struct((wide, width // 2)),
        ],
        compiler_params=params(36),
        cost_estimate=cost(2 * rows * width * wide, 16e6),
        name="root_stage",
    )(ints, *tables, grad, pre, norm, features)


def input_kernel(low, reducer, grad, out):
    half = grad[...].astype(jnp.float32) * 0.5
    out[...] = (dot_cols(low[...], reducer[...]) + half).astype(jnp.bfloat16)


def input_stage(low, reducer, grad, tiles=4):
    rows, width = low.shape
    wide = reducer.shape[0]
    tile = wide // tiles
    return pl.pallas_call(
        input_kernel,
        grid=(tiles,),
        in_specs=[
            pl.BlockSpec((rows, width), lambda i: (0, 0)),
            pl.BlockSpec((tile, width), lambda i: (i, 0)),
            pl.BlockSpec((rows, tile), lambda i: (0, i)),
        ],
        out_specs=pl.BlockSpec((rows, tile), lambda i: (0, i)),
        out_shape=struct((rows, wide), jnp.bfloat16),
        compiler_params=params(30),
        cost_estimate=cost(2 * rows * width * wide, 22e6),
        name="input_stage",
    )(low, reducer, grad)


def halve_stage(ints, pairs, place):
    shapes = [struct(pair[0].shape) for pair in pairs]
    cuts = jax.eval_shape(lambda sums: [item[:2] for item in place(sums)], shapes)

    def kernel(ints, *refs):
        taken, given = refs[: 2 * len(pairs)], refs[2 * len(pairs) :]
        sums = [taken[2 * k][...] + taken[2 * k + 1][...] for k in range(len(pairs))]
        for k, (first, second, bit) in enumerate(place(sums)):
            lower = ints[3 + bit] == 0
            given[2 * k][...] = jnp.where(lower, second, first)
            given[2 * k + 1][...] = jnp.where(lower, first, second)

    out = [struct(half.shape) for item in cuts for half in item]
    return pl.pallas_call(
        kernel,
        in_specs=[SM] + [VM] * (2 * len(pairs)),
        out_specs=[VM] * len(out),
        out_shape=out,
        compiler_params=params(24),
        cost_estimate=cost(0, 4 * sum(half.size for half in out)),
        name="halve_stage",
    )(ints, *[value for pair in pairs for value in pair])


def order_stage(ints, pairs, bits, together):
    rows = [pair[0].shape[0] for pair in pairs]
    width = pairs[0][0].shape[1]

    def kernel(ints, *refs):
        taken, given = refs[: 2 * len(pairs)], refs[2 * len(pairs) :]
        start = 0
        for k, bit in enumerate(bits):
            own, other = taken[2 * k][...], taken[2 * k + 1][...]
            lower = ints[3 + bit] == 0
            out = given[0 if together else k]
            out[start : start + rows[k], :] = jnp.where(lower, own, other)
            out[start + rows[k] : start + 2 * rows[k], :] = jnp.where(lower, other, own)
            start = start + 2 * rows[k] if together else 0

    shapes = [2 * sum(rows)] if together else [2 * count for count in rows]
    return pl.pallas_call(
        kernel,
        in_specs=[SM] + [VM] * (2 * len(pairs)),
        out_specs=[VM] * len(shapes),
        out_shape=[struct((count, width)) for count in shapes],
        compiler_params=params(24),
        cost_estimate=cost(0, 16 * sum(rows) * width),
        name="order_stage",
    )(ints, *[value for pair in pairs for value in pair])


def settle_stage(ints, upper, lower, height, spatial_held):
    width = upper[0].shape[1]
    first = height // 8
    second = upper[0].shape[0] // 4 - first

    def kernel(ints, own, other, own_too, other_too, held, out, out_too):
        mine = jnp.where(pl.program_id(0) < 4, own[...], own_too[...])
        others = jnp.where(pl.program_id(0) < 4, other[...], other_too[...])
        left = jnp.where(ints[3] == 0, mine, others)
        right = jnp.where(ints[3] == 0, others, mine)
        out[:, :width] = left[:first]
        out[:, width:] = right[:first]
        out_too[:, :width] = left[first:]
        out_too[:, width:] = right[first:]

    early = pl.BlockSpec((first + second, width), lambda i: (jnp.minimum(i, 3), 0))
    late = pl.BlockSpec((first + second, width), lambda i: (jnp.maximum(i - 4, 0), 0))
    return pl.pallas_call(
        kernel,
        grid=(8,),
        in_specs=[SM, early, early, late, late, ANY],
        out_specs=[
            pl.BlockSpec((first, 2 * width), lambda i: (i, 0)),
            pl.BlockSpec((second, 2 * width), lambda i: (i, 0)),
        ],
        out_shape=[struct((height, 2 * width)), struct(spatial_held.shape)],
        input_output_aliases={5: 1},
        compiler_params=params(32),
        cost_estimate=cost(0, 32 * upper[0].size),
        name="settle_stage",
    )(ints, *upper, *lower, spatial_held)


def join_blocks(ints, upper, lower, height):
    rows, width = upper[0].shape
    count = rows // height

    def kernel(ints, own, other, own_too, other_too, out):
        step = pl.program_id(0)
        mine = (step // (2 * count)) == ints[3]
        second = (step % (2 * count)) >= count
        for is_mine in (True, False):
            for is_second in (True, False):

                @pl.when((mine == is_mine) & (second == is_second))
                def _():
                    source = (own_too if is_second else own) if is_mine else (
                        other_too if is_second else other
                    )
                    out[...] = source[...]

    spec = pl.BlockSpec((height, width), lambda i: (i % count, 0))
    return pl.pallas_call(
        kernel,
        grid=(4 * count,),
        in_specs=[SM, spec, spec, spec, spec],
        out_specs=pl.BlockSpec((height, width), lambda i: (0, i)),
        out_shape=struct((height, 4 * count * width)),
        compiler_params=params(24),
        cost_estimate=cost(0, 16 * 2 * upper[0].size),
        name="join_blocks",
    )(ints, *upper, *lower)


def lower_kernel(lower, out, held, sems):
    tile = held.shape[1]
    count = held.shape[0]
    first = out.shape[0] - lower.shape[0]
    comes, goes = [], []
    for k in range(count):
        start = k * tile
        comes.append(
            pltpu.make_async_copy(lower.at[pl.ds(start, tile), :], held.at[k], sems.at[0, k])
        )
        goes.append(
            pltpu.make_async_copy(held.at[k], out.at[pl.ds(first + start, tile), :], sems.at[1, k])
        )
        comes[k].start()
    for come, go in zip(comes, goes):
        come.wait()
        go.start()
    for go in goes:
        go.wait()


def lower_stage(lower, rows, tile=512):
    width = lower.shape[1]
    count = lower.shape[0] // tile
    return pl.pallas_call(
        lower_kernel,
        in_specs=[ANY],
        out_specs=ANY,
        out_shape=struct((rows, width)),
        scratch_shapes=[
            pltpu.VMEM((count, tile, width), jnp.float32),
            pltpu.SemaphoreType.DMA((2, count)),
        ],
        compiler_params=params(20),
        cost_estimate=cost(0, 8 * rows * width),
        name="lower_stage",
    )(lower)


class Wide:
    def __init__(self, devices):
        self.devices = devices
        self.bits = [1 << k for k in range(devices.bit_length() - 1)]

    def swap(self, value, bit):
        pairs = [(i, i ^ bit) for i in range(self.devices)]
        return lax.ppermute(value, "wide", pairs)

    def place(self, bit):
        return ((lax.axis_index("wide") & bit) != 0).astype(jnp.int32)

    def groups(self, wide_steps):
        rest = self.bits[1:]
        if not wide_steps:
            return [[bit] for bit in self.bits]
        steps = [rest[k : k + 2] for k in range(0, len(rest), 2)]
        return [[self.bits[0]]] + [
            step if len(step) == 1 else [step[0], step[1], step[0] + step[1]] for step in steps
        ]

    def exchange(self, packed, step, job):
        if job is None:
            return [self.swap(packed, bit) for bit in step], None
        function, arrays = job
        packed, arrays = lax.optimization_barrier((packed, arrays()))
        return lax.optimization_barrier(
            ([self.swap(packed, bit) for bit in step], function(*arrays))
        )

    def merge(self, packed, tallies, jobs={}):
        results = {}
        steps = self.groups(True)

        def join(left, right):
            (mean, square, count, tail), (other_mean, other_square, other_count, _) = left, right
            mean, square, count = join_moments(
                (mean, square, count), (other_mean, other_square, other_count)
            )
            return mean, square, count, tail

        for at, step in enumerate(steps):
            others, results[at] = self.exchange(packed, step, jobs.get(at))
            tables = [packed] + others
            if at == len(tallies):
                tallies.append(tables)
            if at == len(steps) - 1:
                return tables, results
            full = packed.shape[0] == 8
            mean, square, count, tail = pair_up(
                [
                    (table[0:2], table[2:4], tally[4:6, : None if full else 1], tally[6:8])
                    for table, tally in zip(tables, tallies[at])
                ],
                join,
            )
            packed = jnp.concatenate([mean, square] + ([count, tail] if full else []), axis=0)

    def total(self, packed, jobs={}, wide_steps=True):
        results = {}
        steps = self.groups(wide_steps)
        for at, step in enumerate(steps):
            others, results[at] = self.exchange(packed, step, jobs.get(at))
            tables = [packed] + others
            if at == len(steps) - 1:
                return tables, results
            packed = pair_up(tables, lambda a, b: a + b)

    def first_round(self, ints, pairs):
        def quarters(sums):
            pieces = []
            for k in range(4):
                parts = []
                for value in sums:
                    rows = value.shape[0] // 4
                    step = rows // 2
                    parts.append([value[k * rows : k * rows + step], value[k * rows + step : (k + 1) * rows]])
                pieces.append(
                    jnp.concatenate([part[h] for h in (0, 1) for part in parts], axis=0)
                    if len(sums) > 1
                    else sums[0][k * rows : (k + 1) * rows]
                )
            return [(pieces[0], pieces[1], 1), (pieces[2], pieces[3], 2)]

        send, keep, send_too, keep_too = halve_stage(ints, pairs, quarters)
        return [keep, keep_too], [(send, 1), (send_too, 2)]

    def second_round(self, ints, keeps, gets):
        pairs = [(keep[part], get[part]) for part in (0, 1) for keep, get in zip(keeps, gets)]

        def place(sums):
            cuts = []
            for at, bit in ((0, 2), (len(keeps), 1)):
                part = sums[at : at + len(keeps)]
                halves = [
                    [value[: value.shape[0] // 2] for value in part],
                    [value[value.shape[0] // 2 :] for value in part],
                ]
                halves = [
                    half[0] if len(half) == 1 else jnp.concatenate(half, axis=0) for half in halves
                ]
                cuts.append((*halves, bit))
            return cuts

        send, keep, send_too, keep_too = halve_stage(ints, pairs, place)
        return [keep, keep_too], [(send, 2), (send_too, 1)]

    def rounds(self, ints, kept, wanted):
        rest = list(range(3, len(self.bits)))
        gets = yield wanted
        send, keep = halve_stage(
            ints, list(zip(kept, gets)), lambda sums: [(sums[0], sums[1], rest[0])]
        )
        (get,) = yield [(send, rest[0])]
        for bit in rest[1:]:

            def place(sums):
                rows = sums[0].shape[0] // 2
                return [(sums[0][:rows], sums[0][rows:], bit)]

            send, keep = halve_stage(ints, [(keep, get)], place)
            (get,) = yield [(send, bit)]
        value = keep + get
        for bit in rest[:0:-1]:
            (get,) = yield [(value, bit)]
            (value,) = order_stage(ints, [(value, get)], [bit], True)
        (get,) = yield [(value, rest[0])]
        lower = ints[3 + rest[0]] == 0
        value, value_too = jnp.where(lower, value, get), jnp.where(lower, get, value)
        get, get_too = yield [(value, 2), (value_too, 1)]
        value, value_too = order_stage(ints, [(value, get), (value_too, get_too)], [2, 1], False)
        return value, value_too

    def last_rounds(self, ints, value, value_too):
        get, get_too = yield [(value, 1), (value_too, 2)]
        value, value_too = order_stage(ints, [(value, get), (value_too, get_too)], [1, 2], False)
        get, get_too = yield [(value, 0), (value_too, 0)]
        return (value, get), (value_too, get_too)

    def send(self, wanted):
        return [self.swap(value, self.bits[bit]) for value, bit in wanted]


class Bulk:
    def __init__(self, wide, steps):
        self.wide = wide
        self.steps = steps
        self.result = None
        self.launch(next(self.steps))

    def launch(self, wanted):
        self.sends = [value for value, _ in wanted]
        self.flight = self.wide.send(wanted)

    def land(self, values):
        if self.result is not None:
            return values
        values, self.flight = lax.optimization_barrier((values, self.flight))
        self.advance()
        return values

    def advance(self):
        try:
            self.launch(self.steps.send(self.flight))
        except StopIteration as stop:
            self.result = stop.value
            self.sends = list(stop.value)


def on_device(
    wide,
    features,
    group_ids,
    reducer,
    spatial,
    expander,
    gain_first,
    bias_first,
    gain_middle,
    bias_middle,
    gain_last,
    bias_last,
    upstream,
):
    rows = features.shape[0]
    group = group_ids[0]
    side = jnp.where(group == 3, 2, 5 + group)
    area = side * side
    ints = jnp.stack(
        [side, (rows // area) * area, (group == 3).astype(jnp.int32)]
        + [wide.place(bit) for bit in wide.bits]
    ).astype(jnp.int32)
    line = lambda values: values[None, :]
    tallies = []
    plus = lambda tables: pair_up(tables, lambda a, b: a + b)

    pre_first, packed = first_stage(ints, features, reducer)
    tables, _ = wide.merge(packed, tallies)
    tally = tables
    low_first, pre_middle, packed, norm_first = middle_stage(
        ints, tables, line(gain_first), line(bias_first), pre_first, spatial
    )
    tables, _ = wide.merge(packed, tallies)
    low_middle, moments_last, norm_middle = last_stage(
        ints, tables, tally, line(gain_middle), line(bias_middle), pre_middle, expander
    )
    tables, done = wide.merge(
        moments_last, tallies, {1: (lambda low: cov_stage(ints, low), lambda: (low_middle,))}
    )
    centred, cov = done[1]
    block_out, grad_summed, part, local, norm_last = head_stage(
        ints, tables, tally, line(gain_last), line(bias_last), low_middle, expander, features,
        upstream,
    )
    feed = lambda: (part,)
    tables, done = wide.total(
        local,
        {
            1: (lambda part: back_stage(part, expander, 0, 2), feed),
            2: (lambda part: back_stage(part, expander, 1, 2), feed),
            3: (lambda part: weight_stage(low_middle, part, 0, 2), feed),
            4: (lambda part: weight_stage(low_middle, part, 1, 2), feed),
        },
        False,
    )
    sums_last = plus(tables)
    grad_middle, packed, scaled, shift = turn_stage(
        ints, tables, local, moments_last, norm_last, expander, centred, done[1], done[2],
        pre_middle, norm_middle,
    )
    store = {}

    def mend(*arrays):
        store["send"], store["kept"] = mend_stage(ints, *arrays)
        return store["kept"]

    def turned(low, send):
        store["other"] = wide.swap(send, wide.bits[0])
        return turned_stage(low)

    def leave(kept, other):
        kept, wanted = wide.first_round(ints, [(kept, other)])
        store["flight"] = (kept, wide.send(wanted))
        return [value for value, _ in wanted]

    tables, done = wide.total(
        packed,
        {
            1: (mend, lambda: (done[3], done[4], cov, scaled, shift, low_middle)),
            2: (turned, lambda: (low_first, store["send"])),
            3: (leave, lambda: (store["kept"], store["other"])),
        },
        False,
    )
    sums_early = [plus(tables), sums_last]
    rounded, send, kept, spatial_part = taps_stage(
        ints, tables, grad_middle, pre_middle, norm_middle, done[2]
    )
    (rounded, spatial_part), flight = lax.optimization_barrier(
        ((rounded, spatial_part), store["flight"])
    )
    spatial_rest = lax.psum(spatial_part, "wide")

    def finish(rounded, flight, kept_too, send_too):
        other_too = wide.swap(send_too, wide.bits[0])
        kept, wanted = wide.second_round(ints, [flight[0]], [flight[1]])
        rounded, _ = lax.optimization_barrier((rounded, wanted[0][0]))
        bulk_last = Bulk(wide, wide.rounds(ints, kept, wanted))
        grad_first, packed = down_stage(ints, rounded, spatial, pre_first, norm_first)
        packed, bulk_last.flight, other_too = lax.optimization_barrier(
            (packed, bulk_last.flight, other_too)
        )
        def third(*flight):
            store["wanted"] = bulk_last.steps.send(flight)
            return [value for value, _ in store["wanted"]]

        tables, done = wide.total(packed, {1: (third, lambda: bulk_last.flight)})
        tables, sends = lax.optimization_barrier((tables, done[1]))
        bulk_last.launch([(value, bit) for value, (_, bit) in zip(sends, store["wanted"])])
        sums = [plus(tables), *sums_early]
        sums = [(table[2] + table[3], table[0] + table[1]) for table in sums]
        low_grad, send, kept = root_stage(
            ints, tables, grad_first, pre_first, norm_first, features
        )
        other = wide.swap(send, wide.bits[0])
        kept, wanted = wide.first_round(ints, [(kept, other), (kept_too, other_too)])
        low_grad, _ = lax.optimization_barrier((low_grad, wanted[0][0]))
        gets = wide.send(wanted)
        features_grad = input_stage(low_grad, reducer, grad_summed)
        bulk_last.flight, features_grad = lax.optimization_barrier(
            (bulk_last.flight, features_grad)
        )
        bulk_last.advance()
        features_grad, _ = lax.optimization_barrier((features_grad, bulk_last.sends))
        gets, features_grad, sums = lax.optimization_barrier((gets, features_grad, sums))
        kept, wanted = wide.second_round(ints, [kept], [gets])
        bulk_first = Bulk(wide, wide.rounds(ints, kept, wanted))
        finished = False
        while bulk_first.result is None:
            features_grad, _ = lax.optimization_barrier((features_grad, bulk_first.sends))
            if bulk_last.result is None:
                bulk_last.flight, features_grad = lax.optimization_barrier(
                    (bulk_last.flight, features_grad)
                )
                bulk_last.advance()
                if bulk_last.result is not None and not finished:
                    finished = True
                    bulk_last = Bulk(wide, wide.last_rounds(ints, *bulk_last.result))
                features_grad, _ = lax.optimization_barrier((features_grad, bulk_last.sends))
            features_grad = bulk_first.land(features_grad)
        while bulk_last.result is None:
            features_grad = bulk_last.land(features_grad)
        expander_grad = join_blocks(ints, *bulk_last.result, expander.shape[0])
        return features_grad, expander_grad, sums, bulk_first.result

    def nothing(rounded, flight, kept_too, send_too):
        width = reducer.shape[1]
        part = reducer.shape[0] + shared * width
        return (
            jnp.zeros(features.shape, jnp.bfloat16),
            jnp.zeros(expander.shape, jnp.float32),
            [(jnp.zeros((count,)), jnp.zeros((count,))) for count in (width, width, features.shape[1])],
            (jnp.zeros((part // 4, lane)), jnp.zeros((part // 4, lane))),
        )

    features_grad, expander_grad, sums, values = lax.cond(
        group >= 0, finish, nothing, rounded, flight, kept, send
    )
    bulk_first = Bulk(wide, wide.last_rounds(ints, *values))
    bulk_first.advance()
    spatial_rest, _ = lax.optimization_barrier((spatial_rest, bulk_first.sends))
    spatial_grad = lower_stage(spatial_rest, spatial.shape[0])
    bulk_first.flight, spatial_grad = lax.optimization_barrier(
        (bulk_first.flight, spatial_grad)
    )
    reducer_grad, spatial_grad = settle_stage(
        ints, *zip(bulk_first.sends, bulk_first.flight), reducer.shape[0], spatial_grad
    )
    return (
        block_out,
        features_grad,
        reducer_grad,
        spatial_grad,
        expander_grad,
        *[row for pair in sums for row in pair],
    )


def solution(mesh):
    wide = Wide(mesh.shape["wide"])
    in_specs = (
        P("wide", None),
        P("wide"),
        P(),
        P(),
        P(),
        P(),
        P(),
        P(),
        P(),
        P(),
        P(),
        P("wide", None),
    )
    out_specs = (P("wide", None), P("wide", None), P(), P(), P(), P(), P(), P(), P(), P(), P())

    def body(*arrays):
        return on_device(wide, *arrays)

    return jax.shard_map(body, mesh=mesh, in_specs=in_specs, out_specs=out_specs, check_vma=False)
```

time: 882 us -> 364 us (0.41)
  blocking collectives: 364 us -> 0 us
  waiting for transfers between devices: 283 us -> 134 us
  Pallas kernels: 0 us -> 123 us
  other arithmetic: 113 us -> 3.06 us
  matrix products: 80.8 us -> 0 us
  starting transfers between devices: 0.04 us -> 80.5 us
  local copies, waits for them, and re-layouts: 16.3 us -> 4.85 us
    psum x9 -> x0, blocking collectives: 364 us -> none  [the longest x3 122 us: stream_stats(): lax.psum((picker[:, None] * first[None, :], picker * count), 'wide')]
    psum x1, waiting for transfers between devices: 283 us -> 0.01 us  [on_device(): spatial_rest = lax.psum(spatial_part, 'wide')]
    ppermute x0 -> x69, waiting for transfers between devices: none -> 134 us  [swap(): return lax.ppermute(value, 'wide', pairs)]
    pallas_call x0 -> x33, Pallas kernels: none -> 123 us  [the longest x1 17.6 us: head_stage(): pl.pallas_call(head_kernel, grid=(tiles,), in_specs=[SM, *[pl.BlockSpec((...]
    dot_general x9 -> x0, matrix products: 80.8 us -> none  [the longest x3 28.3 us: contract_cols(): lax.dot_general(left, right, (((1,), (1,)), ((), ())), preferred_element_...]
    ppermute x0 -> x69, starting transfers between devices: none -> 80.5 us  [swap(): return lax.ppermute(value, 'wide', pairs)]
    reduce_sum x16 -> x0, other arithmetic: 52.1 us -> none  [the longest x2 37.3 us: norm_back(): first = jnp.sum(grad_norm, axis=0)]
    convert_element_type x16 -> x0, other arithmetic: 29.4 us -> none  [the longest x1 10.8 us: on_device(): low_grad_last = grad_pre_last.astype(jnp.bfloat16)]
  transfers between devices with their start and end apart: 1 -> 70, of which waited for: 1 -> 53; matrix products, arithmetic and copies ran while one was open for 1% -> 1% of each run, Pallas kernels for 0% -> 19%
where the time goes in v2:
time: 364 us; the launch traced here: 361 us
  waiting for transfers between devices  134 us (37%)
  Pallas kernels  123 us (34%)
  starting transfers between devices  80.5 us (22%)
  between operations  15.4 us (4%)
  local copies, waits for them, and re-layouts  4.85 us (1%)
    ppermute x69, waiting for transfers between devices, swap(): return lax.ppermute(value, 'wide', pairs)  134 us
    ppermute x69, starting transfers between devices, swap(): return lax.ppermute(value, 'wide', pairs)  80.5 us
    pallas_call x1, Pallas kernels, head_stage(): pl.pallas_call(head_kernel, grid=(tiles,), in_specs=[SM, *[pl.BlockSpec((...  17.6 us
    pallas_call x1, Pallas kernels, taps_stage(): pl.pallas_call(taps_kernel, in_specs=[SM] + [VM] * (len(tables) + 4), out...  13.9 us
    pallas_call x1, Pallas kernels, middle_stage(): pl.pallas_call(middle_kernel, in_specs=[SM] + [VM] * (len(tables) + 3) +...  13.7 us
    pallas_call x1, Pallas kernels, down_stage(): pl.pallas_call(down_kernel, in_specs=[SM] + [VM] * 3 + [HBM], out_specs=[...  12.5 us
    pallas_call x8, Pallas kernels, halve_stage(): pl.pallas_call(kernel, in_specs=[SM] + [VM] * (2 * len(pairs)), out_specs...  8.41 us
    pallas_call x1, Pallas kernels, first_stage(): pl.pallas_call(first_kernel, in_specs=[SM, ANY, ANY], out_specs=[VM, VM],...  7.3 us
  transfers between devices with their start and end apart: 70, of which 53 were waited for; matrix products, arithmetic and copies ran while one was open for 1% of the time, Pallas kernels for 19%

profile of v2, /device:TPU:0, one launch (start us, length us, event | category | flops | bytes accessed | tf_op | source)
XLA Modules:
  0.0 360.9 jit_solution(1643074214703377902)
XLA Ops:
  8.0 7.3 %first_stage.1 = (f32[1536,512]{1,0:T(8,128)S(1)}, f32[8,512]{1,0:T(8,128)S(1)}) custom-call(s32[8]{0:T(128)S(1)} %stack.45.ints, bf16[1536,2048]{1,0:T(8,128)(2,1)} %refs_12_.1, bf16[2048,512]{1,0:T(8,128)(2,1)} %reducer.1), custom_call_target="tpu_custom_call" | custom-call | flops 3221225472 | bytes 12000000 | tf_op jit(solution)/shard_map/first_stage/pallas_call | solution.py:168
  16.7 3.9 %collective-permute-start.34 = (f32[8,512]{1,0:T(8,128)S(1)}, f32[8,512]{1,0:T(8,128)S(1)}, u32[]{:S(2)}, u32[]{:S(2)}) collective-permute-start(f32[8,512]{1,0:T(8,128)S(1)} %pad_maximum_fusion.3), channel_id=1, source_target_pairs={{0,6},{1,7},{2,4},{3,5},{4,2},{5,3},{6,0},{7,1},{8,14},{9,15},{10,... | collective-permute-start | bytes 49160 | tf_op jit(solution)/shard_map/ppermute | solution.py:979
  22.3 2.0 collective-permute-done.33
  24.9 3.7 %collective-permute-start.37 = (f32[8,512]{1,0:T(8,128)S(1)}, f32[8,512]{1,0:T(8,128)S(1)}, u32[]{:S(2)}, u32[]{:S(2)}) collective-permute-start(f32[8,512]{1,0:T(8,128)S(1)} %pad_maximum_fusion.2.refs_0_.refs_4_), channel_id=1, source_target_pairs={{0,24},{1,25},{2,26},{3,27},{4,28},{5,29},{6,30},{7,31},{8,16},{9,... | collective-permute-start | bytes 49160 | tf_op jit(solution)/shard_map/ppermute | solution.py:979
  30.6 2.6 collective-permute-done.36.refs_2_.refs_6_
  33.3 13.7 %middle_stage.1 = (bf16[1536,512]{1,0:T(8,128)(2,1)S(1)}, f32[1536,512]{1,0:T(8,128)S(1)}, f32[4,512]{1,0:T(4,128)S(1)}, f32[8,512]{1,0:T(8,128)S(1)}) custom-call(s32[8]{0:T(128)S(1)} %stack.45.ints, f32[8,512]{1,0:T(8,128)S(1)} %pad_maximum_fusion.2.refs_0_.refs_4_, f32[8,512]{1,0:T(8,128)S(1)} %collective-permute-done.35.refs_1_.refs_5_, ...), custom_call_target="tpu_custom_call" | custom-call | flops 7247757312 | bytes 12000000 | tf_op jit(solution)/shard_map/middle_stage/pallas_call | solution.py:279
  50.3 2.1 collective-permute-start.39
  56.9 2.3 collective-permute-start.42
  61.0 5.3 %last_stage.1 = (bf16[1536,512]{1,0:T(8,128)(2,1)S(1)}, f32[4,2048]{1,0:T(4,128)S(1)}, f32[8,512]{1,0:T(8,128)S(1)}) custom-call(s32[8]{0:T(128)S(1)} %stack.45.ints, f32[4,512]{1,0:T(4,128)S(1)} %pad_maximum_fusion.5.refs_0_, f32[4,512]{1,0:T(4,128)S(1)} %collective-permute-done.42.refs_1_, f32[4,512]{1,0:T(4,128)S(1)} %collective-permute-done.43.refs_2_, ...), custom_call_target="tpu_custom_call" | custom-call | flops 3221225472 | bytes 8000000 | tf_op jit(solution)/shard_map/last_stage/pallas_call | solution.py:322
  67.7 2.5 collective-permute-start.48
  74.8 2.6 collective-permute-start.51
  82.5 17.6 %head_stage.1 = (bf16[1536,2048]{1,0:T(8,128)(2,1)}, bf16[1536,2048]{1,0:T(8,128)(2,1)}, bf16[1536,2048]{1,0:T(8,128)(2,1)S(1)}, f32[4,2048]{1,0:T(4,128)S(1)}, f32[8,2048]{1,0:T(8,128)S(1)}) custom-call(s32[8]{0:T(128)S(1)} %stack.45.ints, f32[4,2048]{1,0:T(4,128)S(1)} %pad_maximum_fusion.1.refs_0_, f32[4,2048]{1,0:T(4,128)S(1)} %collective-permute-done.49.refs_1_, ...), custom_call_target="tpu_custom_call" | custom-call | flops 3221225472 | bytes 32000000 | tf_op jit(solution)/shard_map/head_stage/pallas_call | solution.py:403
  102.1 1.8 back_stage.2.refs_7_
  107.0 1.8 back_stage.3.refs_8_
  110.2 1.8 weight_stage.2.left_weight
  113.5 2.0 collective-permute-start.56
  115.4 1.8 weight_stage.3.right_weight
  118.7 4.4 %turn_stage.1 = (f32[1536,512]{1,0:T(8,128)S(1)}, f32[4,512]{1,0:T(4,128)S(1)}, bf16[512,2048]{1,0:T(8,128)(2,1)S(1)}, f32[1,2048]{1,0:T(1,128)S(1)}) custom-call(s32[8]{0:T(128)S(1)} %stack.45.ints, f32[4,2048]{1,0:T(4,128)S(1)} %add.281.refs_0_, f32[4,2048]{1,0:T(4,128)S(1)} %collective-permute-done.56.refs_1_, f32[4,2048]{1,0:T(4,128)S(1)} %get-tuple-element.280.refs_2_, ...), custom_call_target="tpu_custom_call" | custom-call | flops 2147483648 | bytes 12000000 | tf_op jit(solution)/shard_map/turn_stage/pallas_call | solution.py:557
  124.9 2.7 mend_stage.1
  140.3 13.9 %taps_stage.1 = (bf16[1536,512]{1,0:T(8,128)(2,1)}, f32[1024,256]{1,0:T(8,128)}, f32[1024,256]{1,0:T(8,128)}, f32[3584,512]{1,0:T(8,128)}) custom-call(s32[8]{0:T(128)S(1)} %stack.45.ints, f32[4,512]{1,0:T(4,128)S(1)} %add.285.refs_0_, f32[4,512]{1,0:T(4,128)S(1)} %collective-permute-done.62.refs_1_, f32[1536,512]{1,0:T(8,128)S(1)} %get-tuple-element.326.refs_2_, ...), custom_call_target="tpu_custom_call" | custom-call | flops 7247757312 | bytes 18000000 | tf_op jit(solution)/shard_map/taps_stage/pallas_call | solution.py:686
  155.9 169.7 %conditional.1 = (bf16[1536,2048]{1,0:T(8,128)(2,1)}, f32[512,2048]{1,0:T(8,128)S(1)}, f32[512]{0:T(512)}, f32[512]{0:T(512)}, f32[512]{0:T(512)}, /*index=5*/f3...) conditional(s32[]{:T(128)} %bitcast.19, () %tuple.70, ...), branch_computations={%region_0.1_spmd, %region_1.2_spmd} | conditional | flops 13690648576 | bytes 185244272 | solution.py:1297
  160.9 12.5 %down_stage.1 = (f32[1536,512]{1,0:T(8,128)S(1)}, f32[4,512]{1,0:T(4,128)S(1)}) custom-call(s32[8]{0:T(128)S(1)} %get-tuple-element.40.ints, bf16[1536,512]{1,0:T(8,128)(2,1)S(1)} %copy-done.14, f32[1536,512]{1,0:T(8,128)S(1)} %get-tuple-element.50.pre.refs_5_, f32[8,512]{1,0:T(8,128)S(1)} %get-tuple-element.51.norm.refs_6_, ...), custom_call_target="tpu_custom_call" | custom-call | flops 7247757312 | bytes 14000000 | tf_op jit(solution)/shard_map/cond/branch_1_fun/down_stage/pallas_call | solution.py:732
  174.7 1.9 collective-permute-start.6
  183.2 2.1 collective-permute-start.7
  187.3 5.9 %root_stage.1 = (bf16[1536,512]{1,0:T(8,128)(2,1)S(1)}, f32[2048,256]{1,0:T(8,128)S(1)}, f32[2048,256]{1,0:T(8,128)S(1)}) custom-call(s32[8]{0:T(128)S(1)} %get-tuple-element.40.ints, f32[4,512]{1,0:T(4,128)S(1)} %add_add_fusion.1.refs_0_, f32[4,512]{1,0:T(4,128)S(1)} %collective-permute-done.7.refs_1_, f32[4,512]{1,0:T(4,128)S(1)} %collective-permute-done.8.refs_2_, ...), custom_call_target="tpu_custom_call" | custom-call | flops 3221225472 | bytes 16000000 | tf_op jit(solution)/shard_map/cond/branch_1_fun/root_stage/pallas_call | solution.py:766
  193.9 3.5 collective-permute-done.11.refs_1_
  197.4 1.8 halve_stage.10
  202.7 2.0 collective-permute-start.10
  205.3 5.8 %input_stage.1 = bf16[1536,2048]{1,0:T(8,128)(2,1)} custom-call(bf16[1536,512]{1,0:T(8,128)(2,1)S(1)} %get-tuple-element.82.low, bf16[2048,512]{1,0:T(8,128)(2,1)S(1)} %copy-done.9, bf16[1536,2048]{1,0:T(8,128)(2,1)S(1)} %bitcast.29), custom_call_target="tpu_custom_call" | custom-call | flops 3221225472 | bytes 22000000 | tf_op jit(solution)/shard_map/cond/branch_1_fun/input_stage/pallas_call | solution.py:802
  211.1 2.1 collective-permute-done.10.refs_1_
  213.8 10.0 %collective-permute-done.14.refs_3_ = f32[768,256]{1,0:T(8,128)S(1)} collective-permute-done((f32[768,256]{1,0:T(8,128)S(1)}, f32[768,256]{1,0:T(8,128)S(1)}, u32[]{:S(2)}, u32[]{:S(2)}) %collective-permute-start.14) | collective-permute-done | bytes 786464 | tf_op jit(solution)/shard_map/cond/branch_1_fun/ppermute | solution.py:979
  228.9 6.6 %collective-permute-done.12 = f32[128,256]{1,0:T(8,128)S(1)} collective-permute-done((f32[128,256]{1,0:T(8,128)S(1)}, f32[128,256]{1,0:T(8,128)S(1)}, u32[]{:S(2)}, u32[]{:S(2)}) %collective-permute-start.12) | collective-permute-done | bytes 131104 | tf_op jit(solution)/shard_map/cond/branch_1_fun/ppermute | solution.py:979
  235.4 1.9 collective-permute-done.16.refs_1_
  238.1 2.9 collective-permute-start.19
  241.0 9.8 %collective-permute-done.15.refs_1_ = f32[128,256]{1,0:T(8,128)S(1)} collective-permute-done((f32[128,256]{1,0:T(8,128)S(1)}, f32[128,256]{1,0:T(8,128)S(1)}, u32[]{:S(2)}, u32[]{:S(2)}) %collective-permute-start.15) | collective-permute-done | bytes 131104 | tf_op jit(solution)/shard_map/cond/branch_1_fun/ppermute | solution.py:979
  253.8 5.3 %collective-permute-done.18 = f32[256,256]{1,0:T(8,128)S(1)} collective-permute-done((f32[256,256]{1,0:T(8,128)S(1)}, f32[256,256]{1,0:T(8,128)S(1)}, u32[]{:S(2)}, u32[]{:S(2)}) %collective-permute-start.18) | collective-permute-done | bytes 262176 | tf_op jit(solution)/shard_map/cond/branch_1_fun/ppermute | solution.py:979
  259.1 4.9 %collective-permute-start.21 = (f32[256,256]{1,0:T(8,128)S(1)}, f32[256,256]{1,0:T(8,128)S(1)}, u32[]{:S(2)}, u32[]{:S(2)}) collective-permute-start(f32[256,256]{1,0:T(8,128)S(1)} %get-tuple-element.378.refs_2_), channel_id=1, source_target_pairs={{0,2},{1,3},{2,0},{3,1},{4,6},{5,7},{6,4},{7,5},{8,10},{9,11},{10,... | collective-permute-start | bytes 786440 | tf_op jit(solution)/shard_map/cond/branch_1_fun/ppermute | solution.py:979
  264.0 4.7 %collective-permute-start.22 = (f32[192,256]{1,0:T(8,128)S(1)}, f32[192,256]{1,0:T(8,128)S(1)}, u32[]{:S(2)}, u32[]{:S(2)}) collective-permute-start(f32[192,256]{1,0:T(8,128)S(1)} %get-tuple-element.119), channel_id=1, source_target_pairs={{0,16},{1,17},{2,18},{3,19},{4,20},{5,21},{6,22},{7,23},{8,24},{9,... | collective-permute-start | bytes 589832 | tf_op jit(solution)/shard_map/cond/branch_1_fun/ppermute | solution.py:979
  268.7 9.7 %collective-permute-done.22 = f32[192,256]{1,0:T(8,128)S(1)} collective-permute-done((f32[192,256]{1,0:T(8,128)S(1)}, f32[192,256]{1,0:T(8,128)S(1)}, u32[]{:S(2)}, u32[]{:S(2)}) %collective-permute-start.22) | collective-permute-done | bytes 196640 | tf_op jit(solution)/shard_map/cond/branch_1_fun/ppermute | solution.py:979
  279.2 3.6 collective-permute-start.24
  282.7 9.5 %collective-permute-done.25.refs_1_ = f32[192,256]{1,0:T(8,128)S(1)} collective-permute-done((f32[192,256]{1,0:T(8,128)S(1)}, f32[192,256]{1,0:T(8,128)S(1)}, u32[]{:S(2)}, u32[]{:S(2)}) %collective-permute-start.25) | collective-permute-done | bytes 196640 | tf_op jit(solution)/shard_map/cond/branch_1_fun/ppermute | solution.py:979
  292.8 2.1 collective-permute-start.28
  296.2 12.3 %collective-permute-done.28 = f32[384,256]{1,0:T(8,128)S(1)} collective-permute-done((f32[384,256]{1,0:T(8,128)S(1)}, f32[384,256]{1,0:T(8,128)S(1)}, u32[]{:S(2)}, u32[]{:S(2)}) %collective-permute-start.28) | collective-permute-done | bytes 393248 | tf_op jit(solution)/shard_map/cond/branch_1_fun/ppermute | solution.py:979
  311.0 12.2 %collective-permute-done.30.refs_3_ = f32[384,256]{1,0:T(8,128)S(1)} collective-permute-done((f32[384,256]{1,0:T(8,128)S(1)}, f32[384,256]{1,0:T(8,128)S(1)}, u32[]{:S(2)}, u32[]{:S(2)}) %collective-permute-start.30) | collective-permute-done | bytes 393248 | tf_op jit(solution)/shard_map/cond/branch_1_fun/ppermute | solution.py:979
  326.9 11.3 %collective-permute-done.65.refs_1_ = f32[768,256]{1,0:T(8,128)S(1)} collective-permute-done((f32[768,256]{1,0:T(8,128)S(1)}, f32[768,256]{1,0:T(8,128)S(1)}, u32[]{:S(2)}, u32[]{:S(2)}) %collective-permute-start.65) | collective-permute-done | bytes 786464 | tf_op jit(solution)/shard_map/ppermute | solution.py:979
  340.2 3.1 copy-done.1
  343.3 3.6 lower_stage.1.held
  346.9 6.9 %settle_stage.1 = (f32[2048,512]{1,0:T(8,128)}, f32[4608,512]{1,0:T(8,128)}) custom-call(s32[8]{0:T(128)S(1)} %stack.45.ints, f32[1536,256]{1,0:T(8,128)S(1)} %get-tuple-element.344.own, f32[1536,256]{1,0:T(8,128)} %collective-permute-done.67.other, f32[1536,256]{1,0:T(8,128)S(1)} %get-tuple-element.345.own_too, ...), custom_call_target="tpu_custom_call", output_to_operand_aliasing={{1}: (5, {})} | custom-call | bytes 12582912 | tf_op jit(solution)/shard_map/settle_stage/pallas_call | solution.py:886
  (207 shorter events, 91.1 us)
Async XLA Ops:
  7.2 333.0 %all-reduce.2.cloned.1.call-start = ((), (), s32[]{:S(2)}) async-start(), calls=%async_computation | async-start | bytes 14680064 | tf_op jit(solution)/shard_map/psum | solution.py:1233
  16.7 5.6 %collective-permute-start.34 = (f32[8,512]{1,0:T(8,128)S(1)}, f32[8,512]{1,0:T(8,128)S(1)}, u32[]{:S(2)}, u32[]{:S(2)}) collective-permute-start(f32[8,512]{1,0:T(8,128)S(1)} %pad_maximum_fusion.3), channel_id=1, source_target_pairs={{0,6},{1,7},{2,4},{3,5},{4,2},{5,3},{6,0},{7,1},{8,14},{9,15},{10,... | collective-permute-start | bytes 49160 | tf_op jit(solution)/shard_map/ppermute | solution.py:979
  24.9 5.7 %collective-permute-start.37 = (f32[8,512]{1,0:T(8,128)S(1)}, f32[8,512]{1,0:T(8,128)S(1)}, u32[]{:S(2)}, u32[]{:S(2)}) collective-permute-start(f32[8,512]{1,0:T(8,128)S(1)} %pad_maximum_fusion.2.refs_0_.refs_4_), channel_id=1, source_target_pairs={{0,24},{1,25},{2,26},{3,27},{4,28},{5,29},{6,30},{7,31},{8,16},{9,... | collective-permute-start | bytes 49160 | tf_op jit(solution)/shard_map/ppermute | solution.py:979
  28.6 4.6 %collective-permute-start.36 = (f32[8,512]{1,0:T(8,128)S(1)}, f32[8,512]{1,0:T(8,128)S(1)}, u32[]{:S(2)}, u32[]{:S(2)}) collective-permute-start(f32[8,512]{1,0:T(8,128)S(1)} %pad_maximum_fusion.2.refs_0_.refs_4_), channel_id=1, source_target_pairs={{0,16},{1,17},{2,18},{3,19},{4,20},{5,21},{6,22},{7,23},{8,24},{9,... | collective-permute-start | bytes 49160 | tf_op jit(solution)/shard_map/ppermute | solution.py:979
  28.6 4.6 %collective-permute-start.35 = (f32[8,512]{1,0:T(8,128)S(1)}, f32[8,512]{1,0:T(8,128)S(1)}, u32[]{:S(2)}, u32[]{:S(2)}) collective-permute-start(f32[8,512]{1,0:T(8,128)S(1)} %pad_maximum_fusion.2.refs_0_.refs_4_), channel_id=1, source_target_pairs={{0,8},{1,9},{2,10},{3,11},{4,12},{5,13},{6,14},{7,15},{8,0},{9,1},... | collective-permute-start | bytes 49160 | tf_op jit(solution)/shard_map/ppermute | solution.py:979
  48.3 4.6 %collective-permute-start.41 = (f32[4,512]{1,0:T(4,128)S(1)}, f32[4,512]{1,0:T(4,128)S(1)}, u32[]{:S(2)}, u32[]{:S(2)}) collective-permute-start(f32[4,512]{1,0:T(4,128)S(1)} %pad_maximum_fusion.4), channel_id=1, source_target_pairs={{0,6},{1,7},{2,4},{3,5},{4,2},{5,3},{6,0},{7,1},{8,14},{9,15},{10,... | collective-permute-start | bytes 24584 | tf_op jit(solution)/shard_map/ppermute | solution.py:979
  50.3 4.3 %collective-permute-start.39 = (f32[4,512]{1,0:T(4,128)S(1)}, f32[4,512]{1,0:T(4,128)S(1)}, u32[]{:S(2)}, u32[]{:S(2)}) collective-permute-start(f32[4,512]{1,0:T(4,128)S(1)} %pad_maximum_fusion.4), channel_id=1, source_target_pairs={{0,2},{1,3},{2,0},{3,1},{4,6},{5,7},{6,4},{7,5},{8,10},{9,11},{10,... | collective-permute-start | bytes 24584 | tf_op jit(solution)/shard_map/ppermute | solution.py:979
  54.8 5.5 %collective-permute-start.44 = (f32[4,512]{1,0:T(4,128)S(1)}, f32[4,512]{1,0:T(4,128)S(1)}, u32[]{:S(2)}, u32[]{:S(2)}) collective-permute-start(f32[4,512]{1,0:T(4,128)S(1)} %pad_maximum_fusion.5.refs_0_), channel_id=1, source_target_pairs={{0,24},{1,25},{2,26},{3,27},{4,28},{5,29},{6,30},{7,31},{8,16},{9,... | collective-permute-start | bytes 24584 | tf_op jit(solution)/shard_map/ppermute | solution.py:979
  56.3 4.6 %collective-permute-start.43 = (f32[4,512]{1,0:T(4,128)S(1)}, f32[4,512]{1,0:T(4,128)S(1)}, u32[]{:S(2)}, u32[]{:S(2)}) collective-permute-start(f32[4,512]{1,0:T(4,128)S(1)} %pad_maximum_fusion.5.refs_0_), channel_id=1, source_target_pairs={{0,16},{1,17},{2,18},{3,19},{4,20},{5,21},{6,22},{7,23},{8,24},{9,... | collective-permute-start | bytes 24584 | tf_op jit(solution)/shard_map/ppermute | solution.py:979
  67.7 5.3 %collective-permute-start.48 = (f32[4,2048]{1,0:T(4,128)S(1)}, f32[4,2048]{1,0:T(4,128)S(1)}, u32[]{:S(2)}, u32[]{:S(2)}) collective-permute-start(f32[4,2048]{1,0:T(4,128)S(1)} %pad_maximum_fusion), channel_id=1, source_target_pairs={{0,6},{1,7},{2,4},{3,5},{4,2},{5,3},{6,0},{7,1},{8,14},{9,15},{10,... | collective-permute-start | bytes 98312 | tf_op jit(solution)/shard_map/ppermute | solution.py:979
  74.8 6.1 %collective-permute-start.51 = (f32[4,2048]{1,0:T(4,128)S(1)}, f32[4,2048]{1,0:T(4,128)S(1)}, u32[]{:S(2)}, u32[]{:S(2)}) collective-permute-start(f32[4,2048]{1,0:T(4,128)S(1)} %pad_maximum_fusion.1.refs_0_), channel_id=1, source_target_pairs={{0,24},{1,25},{2,26},{3,27},{4,28},{5,29},{6,30},{7,31},{8,16},{9,... | collective-permute-start | bytes 98312 | tf_op jit(solution)/shard_map/ppermute | solution.py:979
  77.4 4.8 %collective-permute-start.50 = (f32[4,2048]{1,0:T(4,128)S(1)}, f32[4,2048]{1,0:T(4,128)S(1)}, u32[]{:S(2)}, u32[]{:S(2)}) collective-permute-start(f32[4,2048]{1,0:T(4,128)S(1)} %pad_maximum_fusion.1.refs_0_), channel_id=1, source_target_pairs={{0,16},{1,17},{2,18},{3,19},{4,20},{5,21},{6,22},{7,23},{8,24},{9,... | collective-permute-start | bytes 98312 | tf_op jit(solution)/shard_map/ppermute | solution.py:979
  78.3 4.2 %collective-permute-start.49 = (f32[4,2048]{1,0:T(4,128)S(1)}, f32[4,2048]{1,0:T(4,128)S(1)}, u32[]{:S(2)}, u32[]{:S(2)}) collective-permute-start(f32[4,2048]{1,0:T(4,128)S(1)} %pad_maximum_fusion.1.refs_0_), channel_id=1, source_target_pairs={{0,8},{1,9},{2,10},{3,11},{4,12},{5,13},{6,14},{7,15},{8,0},{9,1},... | collective-permute-start | bytes 98312 | tf_op jit(solution)/shard_map/ppermute | solution.py:979
  113.5 5.2 %collective-permute-start.56 = (f32[4,2048]{1,0:T(4,128)S(1)}, f32[4,2048]{1,0:T(4,128)S(1)}, u32[]{:S(2)}, u32[]{:S(2)}) collective-permute-start(f32[4,2048]{1,0:T(4,128)S(1)} %add.281.refs_0_), channel_id=1, source_target_pairs={{0,16},{1,17},{2,18},{3,19},{4,20},{5,21},{6,22},{7,23},{8,24},{9,... | collective-permute-start | bytes 98312 | tf_op jit(solution)/shard_map/ppermute | solution.py:979
  135.8 4.5 %collective-permute-start.62 = (f32[4,512]{1,0:T(4,128)S(1)}, f32[4,512]{1,0:T(4,128)S(1)}, u32[]{:S(2)}, u32[]{:S(2)}) collective-permute-start(f32[4,512]{1,0:T(4,128)S(1)} %add.285.refs_0_), channel_id=1, source_target_pairs={{0,16},{1,17},{2,18},{3,19},{4,20},{5,21},{6,22},{7,23},{8,24},{9,... | collective-permute-start | bytes 24584 | tf_op jit(solution)/shard_map/ppermute | solution.py:979
  137.4 16.8 %collective-permute-start.63 = (f32[512,256]{1,0:T(8,128)S(1)}, f32[512,256]{1,0:T(8,128)S(1)}, u32[]{:S(2)}, u32[]{:S(2)}) collective-permute-start(f32[512,256]{1,0:T(8,128)S(1)} %get-tuple-element.323), channel_id=1, source_target_pairs={{0,2},{1,3},{2,0},{3,1},{4,6},{5,7},{6,4},{7,5},{8,10},{9,11},{10,... | collective-permute-start | bytes 1572872 | tf_op jit(solution)/shard_map/ppermute | solution.py:979
  138.7 15.5 %collective-permute-start.64 = (f32[512,256]{1,0:T(8,128)S(1)}, f32[512,256]{1,0:T(8,128)S(1)}, u32[]{:S(2)}, u32[]{:S(2)}) collective-permute-start(f32[512,256]{1,0:T(8,128)S(1)} %get-tuple-element.324), channel_id=1, source_target_pairs={{0,4},{1,5},{2,6},{3,7},{4,0},{5,1},{6,2},{7,3},{8,12},{9,13},{10,... | collective-permute-start | bytes 1572872 | tf_op jit(solution)/shard_map/ppermute | solution.py:979
  156.3 17.2 %collective-permute-start.2 = (f32[1024,256]{1,0:T(8,128)}, f32[1024,256]{1,0:T(8,128)S(1)}, u32[]{:S(2)}, u32[]{:S(2)}) collective-permute-start(f32[1024,256]{1,0:T(8,128)} %get-tuple-element.55), channel_id=1, source_target_pairs={{0,1},{1,0},{2,3},{3,2},{4,5},{5,4},{6,7},{7,6},{8,9},{9,8},{10,11... | collective-permute-start | bytes 3145736 | tf_op jit(solution)/shard_map/cond/branch_1_fun/ppermute | solution.py:979
  158.2 15.2 %collective-permute-start.1 = (f32[256,256]{1,0:T(8,128)S(1)}, f32[256,256]{1,0:T(8,128)S(1)}, u32[]{:S(2)}, u32[]{:S(2)}) collective-permute-start(f32[256,256]{1,0:T(8,128)S(1)} %get-tuple-element.54), channel_id=1, source_target_pairs={{0,2},{1,3},{2,0},{3,1},{4,6},{5,7},{6,4},{7,5},{8,10},{9,11},{10,... | collective-permute-start | bytes 786440 | tf_op jit(solution)/shard_map/cond/branch_1_fun/ppermute | solution.py:979
  159.4 14.1 %collective-permute-start = (f32[256,256]{1,0:T(8,128)S(1)}, f32[256,256]{1,0:T(8,128)S(1)}, u32[]{:S(2)}, u32[]{:S(2)}) collective-permute-start(f32[256,256]{1,0:T(8,128)S(1)} %get-tuple-element.48), channel_id=1, source_target_pairs={{0,4},{1,5},{2,6},{3,7},{4,0},{5,1},{6,2},{7,3},{8,12},{9,13},{10,... | collective-permute-start | bytes 786440 | tf_op jit(solution)/shard_map/cond/branch_1_fun/ppermute | solution.py:979
  174.7 4.6 %collective-permute-start.6 = (f32[4,512]{1,0:T(4,128)S(1)}, f32[4,512]{1,0:T(4,128)S(1)}, u32[]{:S(2)}, u32[]{:S(2)}) collective-permute-start(f32[4,512]{1,0:T(4,128)S(1)} %add.159), channel_id=1, source_target_pairs={{0,6},{1,7},{2,4},{3,5},{4,2},{5,3},{6,0},{7,1},{8,14},{9,15},{10,... | collective-permute-start | bytes 24584 | tf_op jit(solution)/shard_map/cond/branch_1_fun/ppermute | solution.py:979
  180.9 5.9 %collective-permute-start.9 = (f32[4,512]{1,0:T(4,128)S(1)}, f32[4,512]{1,0:T(4,128)S(1)}, u32[]{:S(2)}, u32[]{:S(2)}) collective-permute-start(f32[4,512]{1,0:T(4,128)S(1)} %add_add_fusion.1.refs_0_), channel_id=1, source_target_pairs={{0,24},{1,25},{2,26},{3,27},{4,28},{5,29},{6,30},{7,31},{8,16},{9,... | collective-permute-start | bytes 24584 | tf_op jit(solution)/shard_map/cond/branch_1_fun/ppermute | solution.py:979
  181.7 5.1 %collective-permute-start.8 = (f32[4,512]{1,0:T(4,128)S(1)}, f32[4,512]{1,0:T(4,128)S(1)}, u32[]{:S(2)}, u32[]{:S(2)}) collective-permute-start(f32[4,512]{1,0:T(4,128)S(1)} %add_add_fusion.1.refs_0_), channel_id=1, source_target_pairs={{0,16},{1,17},{2,18},{3,19},{4,20},{5,21},{6,22},{7,23},{8,24},{9,... | collective-permute-start | bytes 24584 | tf_op jit(solution)/shard_map/cond/branch_1_fun/ppermute | solution.py:979
  193.2 4.2 %collective-permute-start.11 = (f32[2048,256]{1,0:T(8,128)S(1)}, f32[2048,256]{1,0:T(8,128)S(1)}, u32[]{:S(2)}, u32[]{:S(2)}) collective-permute-start(f32[2048,256]{1,0:T(8,128)S(1)} %get-tuple-element.78), channel_id=1, source_target_pairs={{0,1},{1,0},{2,3},{3,2},{4,5},{5,4},{6,7},{7,6},{8,9},{9,8},{10,11... | collective-permute-start | bytes 6291464 | tf_op jit(solution)/shard_map/cond/branch_1_fun/ppermute | solution.py:979
  199.3 24.5 %collective-permute-start.14 = (f32[768,256]{1,0:T(8,128)S(1)}, f32[768,256]{1,0:T(8,128)S(1)}, u32[]{:S(2)}, u32[]{:S(2)}) collective-permute-start(f32[768,256]{1,0:T(8,128)S(1)} %get-tuple-element.88), channel_id=1, source_target_pairs={{0,4},{1,5},{2,6},{3,7},{4,0},{5,1},{6,2},{7,3},{8,12},{9,13},{10,... | collective-permute-start | bytes 2359304 | tf_op jit(solution)/shard_map/cond/branch_1_fun/ppermute | solution.py:979
  200.7 24.2 %collective-permute-start.13 = (f32[768,256]{1,0:T(8,128)S(1)}, f32[768,256]{1,0:T(8,128)S(1)}, u32[]{:S(2)}, u32[]{:S(2)}) collective-permute-start(f32[768,256]{1,0:T(8,128)S(1)} %get-tuple-element.81), channel_id=1, source_target_pairs={{0,2},{1,3},{2,0},{3,1},{4,6},{5,7},{6,4},{7,5},{8,10},{9,11},{10,... | collective-permute-start | bytes 2359304 | tf_op jit(solution)/shard_map/cond/branch_1_fun/ppermute | solution.py:979
  202.7 10.5 %collective-permute-start.10 = (f32[256,256]{1,0:T(8,128)S(1)}, f32[256,256]{1,0:T(8,128)S(1)}, u32[]{:S(2)}, u32[]{:S(2)}) collective-permute-start(f32[256,256]{1,0:T(8,128)S(1)} %get-tuple-element.69), channel_id=1, source_target_pairs={{0,8},{1,9},{2,10},{3,11},{4,12},{5,13},{6,14},{7,15},{8,0},{9,1},... | collective-permute-start | bytes 786440 | tf_op jit(solution)/shard_map/cond/branch_1_fun/ppermute | solution.py:979
  225.7 11.6 %collective-permute-start.16 = (f32[384,256]{1,0:T(8,128)S(1)}, f32[384,256]{1,0:T(8,128)S(1)}, u32[]{:S(2)}, u32[]{:S(2)}) collective-permute-start(f32[384,256]{1,0:T(8,128)S(1)} %get-tuple-element.100), channel_id=1, source_target_pairs={{0,4},{1,5},{2,6},{3,7},{4,0},{5,1},{6,2},{7,3},{8,12},{9,13},{10,... | collective-permute-start | bytes 1179656 | tf_op jit(solution)/shard_map/cond/branch_1_fun/ppermute | solution.py:979
  226.3 11.1 %collective-permute-start.17 = (f32[384,256]{1,0:T(8,128)S(1)}, f32[384,256]{1,0:T(8,128)S(1)}, u32[]{:S(2)}, u32[]{:S(2)}) collective-permute-start(f32[384,256]{1,0:T(8,128)S(1)} %get-tuple-element.101), channel_id=1, source_target_pairs={{0,2},{1,3},{2,0},{3,1},{4,6},{5,7},{6,4},{7,5},{8,10},{9,11},{10,... | collective-permute-start | bytes 1179656 | tf_op jit(solution)/shard_map/cond/branch_1_fun/ppermute | solution.py:979
  227.5 7.9 %collective-permute-start.12 = (f32[128,256]{1,0:T(8,128)S(1)}, f32[128,256]{1,0:T(8,128)S(1)}, u32[]{:S(2)}, u32[]{:S(2)}) collective-permute-start(f32[128,256]{1,0:T(8,128)S(1)} %get-tuple-element.87), channel_id=1, source_target_pairs={{0,16},{1,17},{2,18},{3,19},{4,20},{5,21},{6,22},{7,23},{8,24},{9,... | collective-permute-start | bytes 393224 | tf_op jit(solution)/shard_map/cond/branch_1_fun/ppermute | solution.py:979
  238.1 15.1 %collective-permute-start.19 = (f32[384,256]{1,0:T(8,128)S(1)}, f32[384,256]{1,0:T(8,128)S(1)}, u32[]{:S(2)}, u32[]{:S(2)}) collective-permute-start(f32[384,256]{1,0:T(8,128)S(1)} %get-tuple-element.111), channel_id=1, source_target_pairs={{0,8},{1,9},{2,10},{3,11},{4,12},{5,13},{6,14},{7,15},{8,0},{9,1},... | collective-permute-start | bytes 1179656 | tf_op jit(solution)/shard_map/cond/branch_1_fun/ppermute | solution.py:979
  241.0 9.8 %collective-permute-start.15 = (f32[128,256]{1,0:T(8,128)S(1)}, f32[128,256]{1,0:T(8,128)S(1)}, u32[]{:S(2)}, u32[]{:S(2)}) collective-permute-start(f32[128,256]{1,0:T(8,128)S(1)} %add.180.refs_0_), channel_id=1, source_target_pairs={{0,16},{1,17},{2,18},{3,19},{4,20},{5,21},{6,22},{7,23},{8,24},{9,... | collective-permute-start | bytes 393224 | tf_op jit(solution)/shard_map/cond/branch_1_fun/ppermute | solution.py:979
  251.4 7.7 %collective-permute-start.18 = (f32[256,256]{1,0:T(8,128)S(1)}, f32[256,256]{1,0:T(8,128)S(1)}, u32[]{:S(2)}, u32[]{:S(2)}) collective-permute-start(f32[256,256]{1,0:T(8,128)S(1)} %order_stage.6), channel_id=1, source_target_pairs={{0,8},{1,9},{2,10},{3,11},{4,12},{5,13},{6,14},{7,15},{8,0},{9,1},... | collective-permute-start | bytes 786440 | tf_op jit(solution)/shard_map/cond/branch_1_fun/ppermute | solution.py:979
  259.1 19.3 %collective-permute-start.21 = (f32[256,256]{1,0:T(8,128)S(1)}, f32[256,256]{1,0:T(8,128)S(1)}, u32[]{:S(2)}, u32[]{:S(2)}) collective-permute-start(f32[256,256]{1,0:T(8,128)S(1)} %get-tuple-element.378.refs_2_), channel_id=1, source_target_pairs={{0,2},{1,3},{2,0},{3,1},{4,6},{5,7},{6,4},{7,5},{8,10},{9,11},{10,... | collective-permute-start | bytes 786440 | tf_op jit(solution)/shard_map/cond/branch_1_fun/ppermute | solution.py:979
  264.0 14.4 %collective-permute-start.20 = (f32[256,256]{1,0:T(8,128)S(1)}, f32[256,256]{1,0:T(8,128)S(1)}, u32[]{:S(2)}, u32[]{:S(2)}) collective-permute-start(f32[256,256]{1,0:T(8,128)S(1)} %get-tuple-element.379.refs_0_), channel_id=1, source_target_pairs={{0,4},{1,5},{2,6},{3,7},{4,0},{5,1},{6,2},{7,3},{8,12},{9,13},{10,... | collective-permute-start | bytes 786440 | tf_op jit(solution)/shard_map/cond/branch_1_fun/ppermute | solution.py:979
  264.0 14.4 %collective-permute-start.22 = (f32[192,256]{1,0:T(8,128)S(1)}, f32[192,256]{1,0:T(8,128)S(1)}, u32[]{:S(2)}, u32[]{:S(2)}) collective-permute-start(f32[192,256]{1,0:T(8,128)S(1)} %get-tuple-element.119), channel_id=1, source_target_pairs={{0,16},{1,17},{2,18},{3,19},{4,20},{5,21},{6,22},{7,23},{8,24},{9,... | collective-permute-start | bytes 589832 | tf_op jit(solution)/shard_map/cond/branch_1_fun/ppermute | solution.py:979
  279.1 15.8 %collective-permute-start.23 = (f32[512,256]{1,0:T(8,128)S(1)}, f32[512,256]{1,0:T(8,128)S(1)}, u32[]{:S(2)}, u32[]{:S(2)}) collective-permute-start(f32[512,256]{1,0:T(8,128)S(1)} %get-tuple-element.130.refs_0_), channel_id=1, source_target_pairs={{0,2},{1,3},{2,0},{3,1},{4,6},{5,7},{6,4},{7,5},{8,10},{9,11},{10,... | collective-permute-start | bytes 1572872 | tf_op jit(solution)/shard_map/cond/branch_1_fun/ppermute | solution.py:979
  279.2 15.7 %collective-permute-start.24 = (f32[512,256]{1,0:T(8,128)S(1)}, f32[512,256]{1,0:T(8,128)S(1)}, u32[]{:S(2)}, u32[]{:S(2)}) collective-permute-start(f32[512,256]{1,0:T(8,128)S(1)} %get-tuple-element.131.refs_2_), channel_id=1, source_target_pairs={{0,4},{1,5},{2,6},{3,7},{4,0},{5,1},{6,2},{7,3},{8,12},{9,13},{10,... | collective-permute-start | bytes 1572872 | tf_op jit(solution)/shard_map/cond/branch_1_fun/ppermute | solution.py:979
  282.7 9.5 %collective-permute-start.25 = (f32[192,256]{1,0:T(8,128)S(1)}, f32[192,256]{1,0:T(8,128)S(1)}, u32[]{:S(2)}, u32[]{:S(2)}) collective-permute-start(f32[192,256]{1,0:T(8,128)S(1)} %add.181.refs_0_), channel_id=1, source_target_pairs={{0,16},{1,17},{2,18},{3,19},{4,20},{5,21},{6,22},{7,23},{8,24},{9,... | collective-permute-start | bytes 589832 | tf_op jit(solution)/shard_map/cond/branch_1_fun/ppermute | solution.py:979
  292.8 15.7 %collective-permute-start.28 = (f32[384,256]{1,0:T(8,128)S(1)}, f32[384,256]{1,0:T(8,128)S(1)}, u32[]{:S(2)}, u32[]{:S(2)}) collective-permute-start(f32[384,256]{1,0:T(8,128)S(1)} %order_stage.8), channel_id=1, source_target_pairs={{0,8},{1,9},{2,10},{3,11},{4,12},{5,13},{6,14},{7,15},{8,0},{9,1},... | collective-permute-start | bytes 1179656 | tf_op jit(solution)/shard_map/cond/branch_1_fun/ppermute | solution.py:979
  295.6 14.0 %collective-permute-start.26 = (f32[1024,256]{1,0:T(8,128)S(1)}, f32[1024,256]{1,0:T(8,128)S(1)}, u32[]{:S(2)}, u32[]{:S(2)}) collective-permute-start(f32[1024,256]{1,0:T(8,128)S(1)} %get-tuple-element.139.own), channel_id=1, source_target_pairs={{0,1},{1,0},{2,3},{3,2},{4,5},{5,4},{6,7},{7,6},{8,9},{9,8},{10,11... | collective-permute-start | bytes 3145736 | tf_op jit(solution)/shard_map/cond/branch_1_fun/ppermute | solution.py:979
  295.7 13.9 %collective-permute-start.27 = (f32[1024,256]{1,0:T(8,128)S(1)}, f32[1024,256]{1,0:T(8,128)S(1)}, u32[]{:S(2)}, u32[]{:S(2)}) collective-permute-start(f32[1024,256]{1,0:T(8,128)S(1)} %get-tuple-element.140.own_too), channel_id=1, source_target_pairs={{0,1},{1,0},{2,3},{3,2},{4,5},{5,4},{6,7},{7,6},{8,9},{9,8},{10,11... | collective-permute-start | bytes 3145736 | tf_op jit(solution)/shard_map/cond/branch_1_fun/ppermute | solution.py:979
  308.5 14.8 %collective-permute-start.30 = (f32[384,256]{1,0:T(8,128)S(1)}, f32[384,256]{1,0:T(8,128)S(1)}, u32[]{:S(2)}, u32[]{:S(2)}) collective-permute-start(f32[384,256]{1,0:T(8,128)S(1)} %get-tuple-element.376.refs_2_), channel_id=1, source_target_pairs={{0,2},{1,3},{2,0},{3,1},{4,6},{5,7},{6,4},{7,5},{8,10},{9,11},{10,... | collective-permute-start | bytes 1179656 | tf_op jit(solution)/shard_map/cond/branch_1_fun/ppermute | solution.py:979
  309.5 15.1 %collective-permute-start.29 = (f32[384,256]{1,0:T(8,128)S(1)}, f32[384,256]{1,0:T(8,128)S(1)}, u32[]{:S(2)}, u32[]{:S(2)}) collective-permute-start(f32[384,256]{1,0:T(8,128)S(1)} %get-tuple-element.377.refs_0_), channel_id=1, source_target_pairs={{0,4},{1,5},{2,6},{3,7},{4,0},{5,1},{6,2},{7,3},{8,12},{9,13},{10,... | collective-permute-start | bytes 1179656 | tf_op jit(solution)/shard_map/cond/branch_1_fun/ppermute | solution.py:979
  325.6 12.6 %collective-permute-start.65 = (f32[768,256]{1,0:T(8,128)S(1)}, f32[768,256]{1,0:T(8,128)S(1)}, u32[]{:S(2)}, u32[]{:S(2)}) collective-permute-start(f32[768,256]{1,0:T(8,128)S(1)} %get-tuple-element.342.refs_0_), channel_id=1, source_target_pairs={{0,2},{1,3},{2,0},{3,1},{4,6},{5,7},{6,4},{7,5},{8,10},{9,11},{10,... | collective-permute-start | bytes 2359304 | tf_op jit(solution)/shard_map/ppermute | solution.py:979
  326.8 12.0 %collective-permute-start.66 = (f32[768,256]{1,0:T(8,128)S(1)}, f32[768,256]{1,0:T(8,128)S(1)}, u32[]{:S(2)}, u32[]{:S(2)}) collective-permute-start(f32[768,256]{1,0:T(8,128)S(1)} %get-tuple-element.343.refs_2_), channel_id=1, source_target_pairs={{0,4},{1,5},{2,6},{3,7},{4,0},{5,1},{6,2},{7,3},{8,12},{9,13},{10,... | collective-permute-start | bytes 2359304 | tf_op jit(solution)/shard_map/ppermute | solution.py:979
  339.6 7.3 %collective-permute-start.67 = (f32[1536,256]{1,0:T(8,128)S(1)}, f32[1536,256]{1,0:T(8,128)}, u32[]{:S(2)}, u32[]{:S(2)}) collective-permute-start(f32[1536,256]{1,0:T(8,128)S(1)} %get-tuple-element.344.own), channel_id=1, source_target_pairs={{0,1},{1,0},{2,3},{3,2},{4,5},{5,4},{6,7},{7,6},{8,9},{9,8},{10,11... | collective-permute-start | bytes 4718600 | tf_op jit(solution)/shard_map/ppermute | solution.py:979
  339.7 7.2 %collective-permute-start.68 = (f32[1536,256]{1,0:T(8,128)S(1)}, f32[1536,256]{1,0:T(8,128)}, u32[]{:S(2)}, u32[]{:S(2)}) collective-permute-start(f32[1536,256]{1,0:T(8,128)S(1)} %get-tuple-element.345.own_too), channel_id=1, source_target_pairs={{0,1},{1,0},{2,3},{3,2},{4,5},{5,4},{6,7},{7,6},{8,9},{9,8},{10,11... | collective-permute-start | bytes 4718600 | tf_op jit(solution)/shard_map/ppermute | solution.py:979
  (41 other events, 415.5 us)
Sparse Core Ops, SparseCore 0:
  156.0 180.1 all-reduce.1
